TPU v7x, 128 devices: a whole 4x4x4 slice. The times are simulated.
128 devices in a mesh: ctx: 8 (over y, core), exp: 16 (over x, z).
Axes of the slice: x: 4, y: 4, z: 4, core: 2. Of those that a mesh axis runs over, the one named last changes fastest.
Arguments:
- query_rows: bfloat16 [4096, 8192], P('ctx', 'exp'), may hold values from -2 to 2
- key_rows: bfloat16 [4096, 8192], P('ctx', 'exp'), may hold values from -2 to 2
- value_rows: bfloat16 [4096, 8192], P('ctx', 'exp'), may hold values from -6 to 6
- log_decay: float32 [4096, 64], P('ctx', 'exp'), may hold values from -1 to 0, as said below
- attn_gain: float32 [8192], P('exp'), may hold values from 0.1 to 1.9
- out_weight: bfloat16 [8192, 6144], P('exp', 'ctx'), may hold values from -0.0625 to 0.0625
- residual: bfloat16 [4096, 6144], P(('ctx', 'exp')), may hold values from -6 to 6
- ffn_gain: float32 [6144], replicated, may hold values from 0.1 to 1.9
- router: float32 [6144, 16], replicated, may hold values from -0.21875 to 0.21875
- expert_ids: int32 [4096, 2], P('ctx'), may hold values from 0 to 15, all different within a row; in each aligned block of 512 rows (0 to 511, 512 to 1023, ...) at most 80 rows name the same one
- w_gate: bfloat16 [16, 6144, 4608], P('exp', None, 'ctx'), may hold values from -0.078125 to 0.078125
- w_up: bfloat16 [16, 6144, 4608], P('exp', None, 'ctx'), may hold values from -0.078125 to 0.078125
- w_down: bfloat16 [16, 4608, 6144], P('exp', 'ctx'), may hold values from -0.09375 to 0.09375
Outputs:
- mixed: bfloat16 [4096, 6144], P(('ctx', 'exp'))
Inputs may be any that keep to these rules, and one draw needn't show every extreme that they name: `expert_ids`: each row names two different experts. Within the 512 rows of each block no expert is named by more than 80 rows, and in some block one expert is named by exactly 80. `log_decay`: strictly negative.
All inputs are finite; a program needn't handle non-finite values.
Results may differ from a plain program's by a relative error of at most 0.024.
Values may be sent and summed in bfloat16 or wider, within the bound.
A program may use at most 128 MiB of HBM per device.

v0:
```python
import jax
import jax.numpy as jnp
from jax import lax
from jax.sharding import PartitionSpec as P


def prefix(array, axis, join, neutral):
    place = lax.axis_index(axis)
    gathered = jax.tree.map(
        lambda a, kind: lax.all_gather(a.astype(kind), axis), array, (jnp.bfloat16, jnp.bfloat16)
    )
    state = jax.tree.map(lambda a, e: jnp.zeros_like(a) + jnp.asarray(e, a.dtype), array, neutral)

    def one(lap, state):
        return join(
            state,
            jax.tree.map(
                lambda a, own: lax.dynamic_index_in_dim(a, lap, 0, False).astype(own.dtype),
                gathered,
                array,
            ),
        )

    return lax.fori_loop(0, place, one, state)


def head_norm(values, gain):
    squares = jnp.mean(values * values, axis=-1, keepdims=True)
    scaled = values * lax.rsqrt(squares + 1e-06) * gain.reshape(1, values.shape[1], -1)
    return scaled.astype(jnp.bfloat16).reshape(values.shape[0], -1)


def row_norm(rows, gain):
    values = rows.astype(jnp.float32)
    squares = jnp.mean(values * values, axis=-1, keepdims=True)
    return (values * lax.rsqrt(squares + 1e-05) * gain).astype(jnp.bfloat16)


def chain_step(earlier, later):
    return (earlier[0] + later[0], jnp.exp(later[0])[:, None, None] * earlier[1] + later[1])


def per_device(
    query_rows,
    key_rows,
    value_rows,
    log_decay,
    attn_gain,
    out_weight,
    residual,
    ffn_gain,
    router,
    expert_ids,
    w_gate,
    w_up,
    w_down,
):
    length = query_rows.shape[0]
    heads = log_decay.shape[1]
    queries = query_rows.reshape(length, heads, -1)
    keys_all = key_rows.reshape(length, heads, -1)
    values_all = value_rows.reshape(length, heads, -1)
    running = jnp.cumsum(log_decay, axis=0)
    later_pos = lax.broadcasted_iota(jnp.int32, (length, length), 0)
    earlier_pos = lax.broadcasted_iota(jnp.int32, (length, length), 1)
    spread = jnp.transpose(running)[:, :, None] - jnp.transpose(running)[:, None, :]
    decay = jnp.where((later_pos >= earlier_pos)[None], jnp.exp(jnp.minimum(spread, 0.0)), 0.0)
    scores = jnp.einsum("thd,shd->hts", queries, keys_all, preferred_element_type=jnp.float32)
    weights = (scores * decay).astype(jnp.bfloat16)
    inner = jnp.einsum("hts,shd->thd", weights, values_all, preferred_element_type=jnp.float32)
    to_end = jnp.exp(running[-1][None, :] - running)
    decayed_keys = (keys_all.astype(jnp.float32) * to_end[:, :, None]).astype(jnp.bfloat16)
    own_state = jnp.einsum(
        "shd,she->hde", decayed_keys, values_all, preferred_element_type=jnp.float32
    )
    block_decay = running[-1]
    identity = (jnp.zeros_like(block_decay), jnp.zeros_like(own_state))
    carried = prefix((block_decay, own_state), "ctx", chain_step, identity)[1]
    scaled_query = queries.astype(jnp.float32) * jnp.exp(running)[:, :, None]
    cross = jnp.einsum("thd,hde->the", scaled_query, carried, precision=lax.Precision.HIGHEST)
    attn_out = head_norm(inner + cross, attn_gain)
    out_full = lax.all_gather(out_weight, "ctx", axis=1, tiled=True)
    summed = lax.psum_scatter(
        jnp.dot(attn_out, out_full, preferred_element_type=jnp.float32).astype(jnp.bfloat16),
        "exp",
        scatter_dimension=0,
        tiled=True,
    ).astype(jnp.float32)
    hidden_rows = (residual.astype(jnp.float32) + summed).astype(jnp.bfloat16)
    normed = lax.all_gather(row_norm(hidden_rows, ffn_gain), "exp", axis=0, tiled=True)
    experts = router.shape[1]
    logits = jnp.dot(normed.astype(jnp.float32), router, precision=lax.Precision.HIGHEST)
    table = expert_ids[:, :, None] == jnp.arange(experts, dtype=jnp.int32)[None, None, :]
    chosen = jnp.sum(jnp.where(table, logits[:, None, :], 0.0), axis=-1)
    gates = jax.nn.sigmoid(chosen)
    shares = gates / jnp.sum(gates, axis=1, keepdims=True)
    owner = lax.axis_index("exp")
    match = expert_ids == owner
    picked = jnp.any(match, axis=1).astype(jnp.int32)
    rank = jnp.cumsum(picked, dtype=jnp.int32) - picked
    mine = jnp.sum(jnp.where(match, shares, 0.0), axis=1)
    capacity = length * 5 // (2 * experts)
    slots = lax.broadcasted_iota(jnp.int32, (capacity, length), 0)
    slot_table = ((rank[None, :] == slots) & (picked[None, :] > 0)).astype(jnp.bfloat16)
    dispatched = jnp.dot(slot_table, normed, preferred_element_type=jnp.float32).astype(
        jnp.bfloat16
    )
    gate_cols = w_gate[0]
    up_cols = w_up[0]
    down_part = w_down[0]
    piece = lax.all_gather(dispatched, "ctx", axis=0, tiled=True)
    gate = jnp.dot(piece, gate_cols, preferred_element_type=jnp.float32)
    upper = jnp.dot(piece, up_cols, preferred_element_type=jnp.float32)
    activated = (jax.nn.silu(gate) * upper).astype(jnp.bfloat16)
    partial_out = jnp.dot(activated, down_part, preferred_element_type=jnp.float32)
    expert_out = lax.psum_scatter(
        partial_out.astype(jnp.bfloat16), "ctx", scatter_dimension=0, tiled=True
    )
    returned_output = lax.dot_general(
        slot_table, expert_out, (((0,), (0,)), ((), ())), preferred_element_type=jnp.float32
    )
    mixture = lax.psum_scatter(
        (returned_output * mine[:, None]).astype(jnp.bfloat16),
        "exp",
        scatter_dimension=0,
        tiled=True,
    ).astype(jnp.float32)
    return (hidden_rows.astype(jnp.float32) + mixture).astype(jnp.bfloat16)


def solution(mesh):
    return jax.shard_map(
        per_device,
        mesh=mesh,
        in_specs=(
            P("ctx", "exp"),
            P("ctx", "exp"),
            P("ctx", "exp"),
            P("ctx", "exp"),
            P("exp"),
            P("exp", "ctx"),
            P(("ctx", "exp"), None),
            P(),
            P(),
            P("ctx", None),
            P("exp", None, "ctx"),
            P("exp", None, "ctx"),
            P("exp", "ctx", None),
        ),
        out_specs=P(("ctx", "exp"), None),
        check_vma=False,
    )
```

profile of v0, /device:TPU:0, one launch (start us, length us, event | category | flops | bytes accessed | tf_op | source)
XLA Modules:
  0.0 463.3 jit_solution(9214042018881505473)
XLA Ops:
  6.5 0.8 reshape.119
  7.3 1.2 reduce-window.15
  8.5 0.2 slice_reduce_fusion
  8.7 0.2 reduce-window.16
  8.9 0.2 slice_reduce_fusion.2
  9.2 1.3 copy.83
  10.5 2.0 convolution_convert_fusion.3
  12.5 0.7 all-gather.7.cloned.1.call-update
  13.3 0.2 fusion.40
  13.5 10.8 %all-gather.1 = bf16[8,1,4]{2,1,0:T(2,128)(2,1)S(1)} all-gather(bf16[1,1,4]{2,1,0:T(2,128)(2,1)S(1)} %bitcast.108), channel_id=1, replica_groups=mesh['ctx'=8,'exp'=16] {'ctx'}, dimensions={0}, use_global_device_ids=true | all-gather | bytes 72 | tf_op jit(solution)/shard_map/all_gather | solution.py:10
  24.6 3.0 fusion.12
  27.7 10.9 %all-gather.13.cloned.1.call-done = bf16[32,128,128]{2,1,0:T(8,128)(2,1)} async-done(((bf16[4,128,128]{2,1,0:T(8,128)(2,1)}), bf16[32,128,128]{2,1,0:T(8,128)(2,1)}) %all-gather.13.cloned.1.call-update) | async-done | bytes 1048592 | tf_op jit(solution)/shard_map/all_gather | solution.py:10
  38.6 1.4 multiply_reduce_fusion
  40.2 40.9 %all-gather.7.cloned.1.call-done = bf16[512,6144]{1,0:T(8,128)(2,1)} async-done(((bf16[512,768]{1,0:T(8,128)(2,1)}), bf16[512,6144]{1,0:T(8,128)(2,1)}) %all-gather.7.cloned.1.call-update) | async-done | bytes 6291472 | tf_op jit(solution)/shard_map/all_gather | solution.py:82
  81.0 8.1 %convolution_convert_fusion.1 = bf16[512,6144]{1,0:T(8,128)(2,1)} fusion(bf16[512,512]{0,1:T(8,128)(2,1)S(1)} %bitcast.97, bf16[512,6144]{1,0:T(8,128)(2,1)} %all-gather.7.cloned.1.call-done), kind=kOutput, calls=%fused_computation.4 | convolution fusion | flops 3224371200 | bytes 13107200 | tf_op jit(solution)/shard_map/dot_general | solution.py:84
  89.2 81.8 %reduce-scatter.4.cloned.1.call-done = bf16[32,6144]{1,0:T(8,128)(2,1)} async-done(((bf16[512,6144]{1,0:T(8,128)(2,1)}), bf16[32,6144]{1,0:T(8,128)(2,1)}) %reduce-scatter.4.cloned.1.call-update) | async-done | bytes 393232 | tf_op jit(solution)/shard_map/reduce_scatter | solution.py:83
  170.9 1.2 fusion.16
  172.2 1.9 fusion.18
  174.2 0.3 reduce-window.19
  174.8 60.1 %all-gather.9.cloned.1.call-done = bf16[512,6144]{1,0:T(8,128)(2,1)} async-done(((bf16[32,6144]{1,0:T(8,128)(2,1)}), bf16[512,6144]{1,0:T(8,128)(2,1)}) %all-gather.9.cloned.1.call-update) | async-done | bytes 6291472 | tf_op jit(solution)/shard_map/all_gather | solution.py:90
  234.9 4.9 %convolution_convert_fusion.2 = bf16[80,6144]{1,0:T(8,128)(2,1)} fusion(bf16[512,6144]{1,0:T(8,128)(2,1)} %all-gather.9.cloned.1.call-done, s32[512]{0:T(512)S(1)} %convert_subtract_fusion, pred[512]{0:T(512)(128)(4,1)S(1)} %get-tuple-element.94), kind=kOutput, calls=%fused_computation.10 | convolution fusion | flops 503889920 | bytes 7277056 | tf_op jit(solution)/shard_map/dot_general | solution.py:105
  239.9 0.2 reduce-scatter.6.cloned.1.call-start
  240.1 47.0 %all-gather.11.cloned.1.call-done = bf16[640,6144]{1,0:T(8,128)(2,1)} async-done(((bf16[80,6144]{1,0:T(8,128)(2,1)}), bf16[640,6144]{1,0:T(8,128)(2,1)}) %all-gather.11.cloned.1.call-update) | async-done | bytes 7864336 | tf_op jit(solution)/shard_map/all_gather | solution.py:111
  287.1 10.9 %fusion.3 = f32[640,576]{0,1:T(8,128)S(1)} fusion(bf16[640,6144]{1,0:T(8,128)(2,1)} %all-gather.11.cloned.1.call-done, bf16[1,6144,576]{1,2,0:T(8,128)(2,1)} %param.25), kind=kOutput, calls=%fused_computation.8 | convolution fusion | flops 4529848320 | bytes 16416768 | tf_op jit(solution)/shard_map/dot_general | solution.py:112
  298.1 8.5 %fusion.8 = bf16[640,576]{0,1:T(8,128)(2,1)S(1)} fusion(bf16[640,6144]{1,0:T(8,128)(2,1)S(1)} %copy-done.8, bf16[1,6144,576]{1,2,0:T(8,128)(2,1)} %param.26, f32[640,576]{0,1:T(8,128)S(1)} %fusion.3), kind=kOutput, calls=%fused_computation.13 | convolution fusion | flops 4532060160 | bytes 17154048 | tf_op jit(solution)/shard_map/dot_general | solution.py:113
  306.6 10.5 %convolution_convert_fusion = bf16[640,6144]{1,0:T(8,128)(2,1)} fusion(bf16[640,576]{0,1:T(8,128)(2,1)S(1)} %fusion.8, bf16[1,576,6144]{2,1,0:T(8,128)(2,1)} %param.27), kind=kOutput, calls=%fused_computation.3 | convolution fusion | flops 4533780480 | bytes 15679488 | tf_op jit(solution)/shard_map/dot_general | solution.py:115
  317.2 0.9 copy-done.4
  318.1 7.0 %fusion.44 = f32[512,16]{0,1:T(8,128)S(1)} fusion(bf16[512,6144]{1,0:T(8,128)(2,1)} %all-gather.9.cloned.1.call-done, f32[6144,16]{0,1:T(8,128)S(1)} %copy-done.4), kind=kOutput, calls=%fused_computation.73 | convolution fusion | flops 603979776 | bytes 6717440 | tf_op jit(solution)/shard_map/dot_general | solution.py:92
  325.3 42.1 %reduce-scatter.6.cloned.1.call-done = bf16[80,6144]{1,0:T(8,128)(2,1)} async-done(((bf16[640,6144]{1,0:T(8,128)(2,1)}), bf16[80,6144]{1,0:T(8,128)(2,1)}) %reduce-scatter.6.cloned.1.call-update) | async-done | bytes 983056 | tf_op jit(solution)/shard_map/reduce_scatter | solution.py:116
  367.4 5.8 %multiply_convert_fusion = bf16[512,6144]{1,0:T(8,128)(2,1)} fusion(bf16[80,6144]{1,0:T(8,128)(2,1)} %reduce-scatter.6.cloned.1.call-done, f32[512]{0:T(512)S(1)} %fusion.39, s32[512]{0:T(512)S(1)} %convert_subtract_fusion, pred[512]{0:T(512)(128)(4,1)S(1)} %get-tuple-element.94), kind=kOutput, calls=%fused_computation.2 | convolution fusion | flops 509689856 | bytes 7279104 | tf_op jit(solution)/shard_map/dot_general | solution.py:119
  373.2 81.4 %reduce-scatter.8.cloned.1.call-done = bf16[32,6144]{1,0:T(8,128)(2,1)} async-done(((bf16[512,6144]{1,0:T(8,128)(2,1)}), bf16[32,6144]{1,0:T(8,128)(2,1)}) %reduce-scatter.8.cloned.1.call-update) | async-done | bytes 393232 | tf_op jit(solution)/shard_map/reduce_scatter | solution.py:122
  454.6 1.9 fusion.19
  (49 shorter events, 1.4 us)
Async XLA Ops:
  6.5 18.1 %copy-start = (bf16[512,512]{1,0:T(8,128)(2,1)S(1)}, bf16[512,512]{1,0:T(8,128)(2,1)}, u32[]{:S(2)}) copy-start(bf16[512,512]{1,0:T(8,128)(2,1)} %param.15) | copy-start | bytes 1572868
  6.5 32.0 %all-gather.13.cloned.1.call-start = ((), (), s32[]{:S(2)}) async-start(), calls=%async_computation.9 | async-start | bytes 1179648 | tf_op jit(solution)/shard_map/all_gather | solution.py:10
  12.5 68.5 %all-gather.7.cloned.1.call-start = ((), (), s32[]{:S(2)}) async-start(), calls=%async_computation.3 | async-start | bytes 7077888 | tf_op jit(solution)/shard_map/all_gather | solution.py:82
  13.2 157.7 %reduce-scatter.4.cloned.1.call-start = ((), (), s32[]{:S(2)}) async-start(), calls=%async_computation.4 | async-start | bytes 6684672 | tf_op jit(solution)/shard_map/reduce_scatter | solution.py:83
  24.6 15.4 %copy-start.7 = (f32[512]{0:T(512)S(1)}, f32[512]{0:T(512)}, u32[]{:S(2)}) copy-start(f32[512]{0:T(512)} %param.19) | copy-start | bytes 6148
  89.1 81.8 %copy-start.2 = (bf16[32,6144]{1,0:T(8,128)(2,1)S(1)}, bf16[32,6144]{1,0:T(8,128)(2,1)}, u32[]{:S(2)}) copy-start(bf16[32,6144]{1,0:T(8,128)(2,1)} %param.21) | copy-start | bytes 1179652
  89.1 83.1 %copy-start.6 = (f32[6144]{0:T(1024)S(1)}, f32[6144]{0:T(1024)}, u32[]{:S(2)}) copy-start(f32[6144]{0:T(1024)} %param.22) | copy-start | bytes 73732
  89.1 85.1 %copy-start.5 = (s32[512,2]{0,1:T(2,128)S(1)}, s32[512,2]{0,1:T(2,128)}, u32[]{:S(2)}) copy-start(s32[512,2]{0,1:T(2,128)} %param.24) | copy-start | bytes 12292
  89.1 145.8 %all-gather.9.cloned.1.call-start = ((), (), s32[]{:S(2)}) async-start(), calls=%async_computation.5 | async-start | bytes 6684672 | tf_op jit(solution)/shard_map/all_gather | solution.py:90
  174.1 113.0 %all-gather.11.cloned.1.call-start = ((), (), s32[]{:S(2)}) async-start(), calls=%async_computation.6 | async-start | bytes 8847360 | tf_op jit(solution)/shard_map/all_gather | solution.py:111
  239.9 127.6 %reduce-scatter.6.cloned.1.call-start = ((), (), s32[]{:S(2)}) async-start(), calls=%async_computation.7 | async-start | bytes 8847360 | tf_op jit(solution)/shard_map/reduce_scatter | solution.py:116
  287.1 10.9 %copy-start.8 = (bf16[640,6144]{1,0:T(8,128)(2,1)S(1)}, bf16[640,6144]{1,0:T(8,128)(2,1)}, u32[]{:S(2)}) copy-start(bf16[640,6144]{1,0:T(8,128)(2,1)} %all-gather.11.cloned.1.call-done) | copy-start | bytes 23592964
  317.1 1.0 copy-start.4
  317.2 137.4 %reduce-scatter.8.cloned.1.call-start = ((), (), s32[]{:S(2)}) async-start(), calls=%async_computation.8 | async-start | bytes 6684672 | tf_op jit(solution)/shard_map/reduce_scatter | solution.py:122
  325.3 129.3 %copy-start.3 = (bf16[32,6144]{1,0:T(8,128)(2,1)S(1)}, bf16[32,6144]{1,0:T(8,128)(2,1)}, u32[]{:S(2)}) copy-start(bf16[32,6144]{1,0:T(8,128)(2,1)} %reduce-scatter.4.cloned.1.call-done) | copy-start | bytes 1179652
  367.4 89.0 %copy-start.1 = (bf16[512,512]{1,0:T(8,128)(2,1)S(1)}, bf16[512,512]{1,0:T(8,128)(2,1)}, u32[]{:S(2)}) copy-start(bf16[512,512]{1,0:T(8,128)(2,1)} %param.15) | copy-start | bytes 1572868
Sparse Core Ops, SparseCore 0:
  12.6 25.8 all-gather.12
  40.2 40.7 all-gather.6
  89.3 81.6 reduce-scatter.3
  174.2 60.6 all-gather.8
  240.0 47.0 all-gather.10
  317.3 50.0 reduce-scatter.5
  373.3 81.1 reduce-scatter.7
where the time goes:
time: 464 us; the launch traced here: 463 us
  waiting for transfers between devices  365 us (79%)
  matrix products  62.3 us (13%)
  between operations  13.6 us (3%)
  blocking collectives  10.8 us (2%)
  other arithmetic  7.34 us (2%)
    reduce_scatter x1, waiting for transfers between devices, per_device(): lax.psum_scatter(jnp.dot(attn_out, out_full, preferred_element_type=jnp.f...  81.8 us
    reduce_scatter x1, waiting for transfers between devices, per_device(): lax.psum_scatter((returned_output * mine[:, None]).astype(jnp.bfloat16),...  81.4 us
    all_gather x1, waiting for transfers between devices, per_device(): lax.all_gather(row_norm(hidden_rows, ffn_gain), 'exp', axis=0, tiled=True)  60.1 us
    all_gather x1, waiting for transfers between devices, per_device(): piece = lax.all_gather(dispatched, 'ctx', axis=0, tiled=True)  47 us
    reduce_scatter x1, waiting for transfers between devices, per_device(): lax.psum_scatter(partial_out.astype(jnp.bfloat16), 'ctx', scatter_dimensi...  42.1 us
    all_gather x1, waiting for transfers between devices, per_device(): out_full = lax.all_gather(out_weight, 'ctx', axis=1, tiled=True)  40.9 us
    dot_general x1, matrix products, per_device(): gate = jnp.dot(piece, gate_cols, preferred_element_type=jnp.float32)  10.9 us
    all_gather x1, waiting for transfers between devices, prefix(): lax.all_gather(a.astype(kind), axis)  10.9 us
  transfers between devices with their start and end apart: 7, of which 7 were waited for; matrix products, arithmetic and copies ran while one was open for 3% of the time, Pallas kernels for 0%

commit v1 on v0

v1 whole, which is shorter than its diff:
```python
import functools

import jax
import jax.numpy as jnp
from jax import lax
from jax.experimental import pallas as pl
from jax.experimental.pallas import tpu as pltpu
from jax.sharding import PartitionSpec as P

MESH = pl.DeviceIdType.MESH
F32 = jnp.float32
BF16 = jnp.bfloat16
EXPERTS = 16
CAP = 80
UNIT = 384
LINKS = 128


def place():
    ctx = lax.axis_index("ctx")
    exp = lax.axis_index("exp")
    return ctx // 2, ctx % 2, exp // 4, exp % 4


def along(axis, step):
    y, core, x, z = place()
    step = step % 4
    if axis == "x":
        return (y * 2 + core, (x + step) % 4 * 4 + z)
    if axis == "z":
        return (y * 2 + core, x * 4 + (z + step) % 4)
    return ((y + step) % 4 * 2 + core, x * 4 + z)


def exp_peer(step):
    return (lax.axis_index("ctx"), (lax.axis_index("exp") + step) % EXPERTS)


def other_core():
    y, core, _, _ = place()
    return (y * 2 + 1 - core, lax.axis_index("exp"))


class Links:
    def __init__(self, send, recv):
        self.send, self.recv, self.count, self.open = send, recv, 0, []

    def copy(self, src, dst, device):
        made = pltpu.make_async_remote_copy(
            src_ref=src,
            dst_ref=dst,
            send_sem=self.send.at[self.count],
            recv_sem=self.recv.at[self.count],
            device_id=device,
            device_id_type=MESH,
        )
        made.start()
        self.count += 1
        self.open.append(made)
        return made

    def drain(self):
        for made in self.open:
            made.wait_send()
        self.open = []


def add_into(target, extra):
    size = 128 if target.shape[0] % 128 == 0 else 80

    def one(i, carry):
        rows = rows_at(i * size, size)
        target[rows, :] = (target[rows, :].astype(F32) + extra[rows, :].astype(F32)).astype(BF16)
        return carry

    lax.fori_loop(0, target.shape[0] // size, one, 0)


class RingSum:
    def __init__(self, links, axis, part, base, n, first, second):
        place_of = dict(zip(("y", "core", "x", "z"), place()))
        self.links, self.axis, self.i = links, axis, place_of[axis]
        self.part, self.base, self.n = part, base, n
        self.first, self.second = first, second

    def low(self, d):
        return self.part.at[rows_at(self.base + d * self.n, self.n // 2)]

    def high(self, d):
        return self.part.at[rows_at(self.base + d * self.n + self.n // 2, self.n // 2)]

    def slot(self, k):
        return pl.ds(k * (self.n // 2), self.n // 2)

    def opposite(self):
        far, slot = (self.i + 2) % 4, self.slot
        up = self.links.copy(self.low(far), self.first.at[slot(0)], along(self.axis, 1))
        down = self.links.copy(self.high(far), self.first.at[slot(1)], along(self.axis, -1))
        self.far = (up, down)

    def direct(self):
        up, down, slot = (self.i + 1) % 4, (self.i + 3) % 4, self.slot
        self.near = [
            self.links.copy(self.high(up), self.second.at[slot(1)], along(self.axis, 1)),
            self.links.copy(self.low(down), self.second.at[slot(2)], along(self.axis, -1)),
        ]

    def relay(self):
        up, down, slot = (self.i + 1) % 4, (self.i + 3) % 4, self.slot
        self.far[0].wait_recv()
        add_into(self.low(up), self.first.at[slot(0)])
        self.near.append(
            self.links.copy(self.low(up), self.second.at[slot(0)], along(self.axis, 1))
        )
        self.far[1].wait_recv()
        add_into(self.high(down), self.first.at[slot(1)])
        self.near.append(
            self.links.copy(self.high(down), self.second.at[slot(3)], along(self.axis, -1))
        )

    def arrived(self):
        for made in self.near:
            made.wait_recv()

    def total(self, start, size):
        own = self.part[rows_at(self.base + self.i * self.n + start, size), :].astype(F32)
        own = own + self.second[rows_at(start, size), :].astype(F32)
        return own + self.second[rows_at(self.n + start, size), :].astype(F32)


def columns(start, size):
    return pl.ds(pl.multiple_of(start, 128), size)


def rows_at(start, size):
    return pl.ds(pl.multiple_of(start, 16), size)


def layer_kernel(
    attn_ref,
    out_w_ref,
    resid_ref,
    ids_ref,
    gain_ref,
    router_ref,
    gate_ref,
    up_ref,
    down_ref,
    out_ref,
    wide,
    gate_up,
    work,
    first_a,
    first_b,
    second_a,
    second_b,
    half_a,
    half_b,
    last_first_a,
    last_first_b,
    last_second_a,
    last_second_b,
    resid_cols,
    hidden,
    table,
    pieces,
    rows_in,
    tokens,
    active,
    partner,
    first_y,
    second_y,
    back,
    mixed,
    rows_out,
    local,
    send,
    recv,
):
    y, core, x, z = place()
    ctx = y * 2 + core
    me = lax.axis_index("exp")
    links = Links(send, recv)

    load_w = pltpu.make_async_copy(out_w_ref, wide.at[:, pl.ds(0, 512)], local.at[0])
    load_w.start()
    load_gate = pltpu.make_async_copy(gate_ref, gate_up.at[pl.ds(0, 576)], local.at[1])
    load_up = pltpu.make_async_copy(up_ref, gate_up.at[pl.ds(576, 576)], local.at[2])

    barrier = pltpu.get_barrier_semaphore()
    for step in range(1, EXPERTS):
        pl.semaphore_signal(barrier, inc=1, device_id=exp_peer(step), device_id_type=MESH)
    for device in (along("y", 1), along("y", -1), other_core()):
        pl.semaphore_signal(barrier, inc=1, device_id=device, device_id_type=MESH)
    pl.semaphore_wait(barrier, EXPERTS + 2)

    resid_moves = []
    for step in range(1, EXPERTS):
        to = (me + step) % EXPERTS
        resid_moves.append(
            links.copy(
                resid_ref.at[:, columns(to * UNIT, UNIT)],
                resid_cols.at[rows_at(me * 32, 32)],
                exp_peer(step),
            )
        )
    resid_cols[rows_at(me * 32, 32), :] = resid_ref[:, columns(me * UNIT, UNIT)]

    load_w.wait()
    load_gate.start()
    load_up.start()

    def keep(base, r, u):
        for half in range(2):
            for side in range(2):
                to = base + (side * 4 + u + half) * 128
                work[rows_at(to, 128), :] = r[
                    side * 128 : side * 128 + 128, half * UNIT : half * UNIT + UNIT
                ].astype(BF16)

    def project_a(to):
        def one(h, carry):
            w = wide[to * 2 + h, pl.ds(0, 512), :]
            r = jnp.dot(attn_ref[pl.ds(0, 256), :], w, preferred_element_type=F32)
            keep(to * 1024, r, h * 2)
            return carry

        lax.fori_loop(0, 2, one, 0)

    def project_b(pair):
        def one(to, carry):
            w = wide[to * 2 + pair, pl.ds(0, 512), :]
            r = jnp.dot(attn_ref[pl.ds(256, 256), :], w, preferred_element_type=F32)
            for half in range(2):
                for side in range(2):
                    start = 4096 + (pair * 2 + half) * 1024 + (side * 4 + to) * 128
                    work[rows_at(start, 128), :] = r[
                        side * 128 : side * 128 + 128, half * UNIT : half * UNIT + UNIT
                    ].astype(BF16)
            return carry

        lax.fori_loop(0, 4, one, 0)

    ring_a = RingSum(links, "x", work, 0, 1024, first_a, second_a)
    ring_b = RingSum(links, "z", work, 4096, 1024, first_b, second_b)
    project_a((x + 2) % 4)
    ring_a.opposite()
    far_pair = (z + 2) % 4 // 2
    project_b(far_pair)
    ring_b.opposite()
    project_a((x + 1) % 4)
    project_a((x + 3) % 4)
    ring_a.direct()
    project_b(1 - far_pair)
    ring_b.direct()
    project_a(x)
    load_down = []
    for s in range(8):
        made = pltpu.make_async_copy(
            down_ref.at[:, pl.ds(s * 768, 768)], wide.at[s], local.at[3 + s]
        )
        made.start()
        load_down.append(made)

    experts = lax.broadcasted_iota(jnp.int32, (EXPERTS, 512), 0)
    picked = (ids_ref[0:1, :] == experts) | (ids_ref[1:2, :] == experts)
    before = lax.broadcasted_iota(jnp.int32, (512, 512), 0) < lax.broadcasted_iota(
        jnp.int32, (512, 512), 1
    )
    rank = jnp.dot(
        jnp.where(picked, 1.0, 0.0).astype(BF16),
        jnp.where(before, 1.0, 0.0).astype(BF16),
        preferred_element_type=F32,
    )
    code = jnp.where(picked, rank, -1.0)
    slots = lax.broadcasted_iota(jnp.int32, (CAP, 512), 0).astype(F32)
    for e in range(EXPERTS):
        table[pl.ds(e * CAP, CAP), :] = jnp.where(code[e : e + 1, :] == slots, 1.0, 0.0).astype(
            BF16
        )

    ring_a.relay()
    ring_b.relay()

    def gather_sum(ring, target):
        ring.arrived()

        def one(u, carry):
            for side in range(2):
                rows = rows_at(u * 256 + side * 128, 128)
                target[rows, :] = ring.total(side * 512 + u * 128, 128).astype(BF16)
            return carry

        lax.fori_loop(0, 4, one, 0)

    last_a = RingSum(links, "z", half_a, 0, 256, last_first_a, last_second_a)
    last_b = RingSum(links, "x", half_b, 0, 256, last_first_b, last_second_b)
    gather_sum(ring_a, half_a)
    last_a.opposite()
    last_a.direct()
    gather_sum(ring_b, half_b)
    last_b.opposite()
    last_b.direct()
    last_a.relay()
    last_b.relay()
    for made in resid_moves:
        made.wait_recv()

    def finish_sum(ring, start):
        ring.arrived()
        rows = pl.ds(start, 256)
        hidden[rows, :] = (ring.total(0, 256) + resid_cols[rows, :].astype(F32)).astype(BF16)

    finish_sum(last_a, 0)
    finish_sum(last_b, 256)

    def rows_for(e):
        t = table[rows_at(e * CAP, CAP), :]
        return jnp.dot(t, hidden[...], preferred_element_type=F32).astype(BF16)

    row_moves = []
    for step in range(1, EXPERTS):
        piece = pl.ds(step * CAP, CAP)
        pieces[piece, :] = rows_for((me + step) % EXPERTS)
        row_moves.append(
            links.copy(
                pieces.at[piece], rows_in.at[:, columns(me * UNIT, UNIT)], exp_peer(step)
            )
        )
    rows_in[:, columns(me * UNIT, UNIT)] = rows_for(me)
    my_table = table[rows_at(me * CAP, CAP), :]
    my_ids = lax.dot_general(
        my_table,
        ids_ref[...].astype(F32).astype(BF16),
        (((1,), (1,)), ((), ())),
        preferred_element_type=F32,
    )
    router_high = router_ref[...].astype(BF16)
    router_low = (router_ref[...] - router_high.astype(F32)).astype(BF16)
    for made in row_moves:
        made.wait_recv()

    links.drain()

    mine = rows_at(ctx * CAP, CAP)
    squares = jnp.zeros((CAP, 1), F32)
    for u in range(EXPERTS):
        part = rows_in[:, pl.ds(u * UNIT, UNIT)].astype(F32)
        squares = squares + jnp.sum(part * part, axis=1, keepdims=True)
    scale = lax.rsqrt(squares / 6144.0 + 1e-05)
    for u in range(EXPERTS):
        cols = pl.ds(u * UNIT, UNIT)
        part = rows_in[:, cols].astype(F32)
        tokens[mine, cols] = (part * scale * gain_ref[:, cols]).astype(BF16)

    low, high = pl.ds(0, 3072), pl.ds(3072, 3072)

    def spread(block, cols, device):
        ref = tokens.at[rows_at(block * CAP, CAP), cols]
        return links.copy(ref, ref, device)

    above, below, far = (y + 1) % 4, (y + 3) % 4, (y + 2) % 4
    pair_own = spread(ctx, pl.ds(0, 6144), other_core())
    up_low = spread(ctx, low, along("y", 1))
    down_high = spread(ctx, high, along("y", -1))
    up_high = spread(ctx, high, along("y", 1))
    down_low = spread(ctx, low, along("y", -1))

    normed = tokens[mine, :]
    turned = (((1,), (1,)), ((), ()))
    logits = lax.dot_general(normed, router_high, turned, preferred_element_type=F32)
    logits = logits + lax.dot_general(normed, router_low, turned, preferred_element_type=F32)
    gates = 1.0 / (1.0 + jnp.exp(-logits))
    lanes = lax.broadcasted_iota(jnp.int32, (CAP, EXPERTS), 1)
    lanes_f = lanes.astype(F32)
    both = (my_ids[:, 0:1] == lanes_f) | (my_ids[:, 1:2] == lanes_f)
    total = jnp.sum(jnp.where(both, gates, 0.0), axis=1, keepdims=True)
    share = jnp.sum(jnp.where(lanes == me, gates, 0.0), axis=1, keepdims=True) / total

    load_gate.wait()
    load_up.wait()
    for made in load_down:
        made.wait()

    def gate_and_up(chip):
        rows = rows_at(chip * (2 * CAP), 2 * CAP)
        r = lax.dot_general(tokens[rows, :], gate_up[...], turned, preferred_element_type=F32)
        gate, upper = r[:, :576], r[:, 576:]
        active[...] = (gate / (1.0 + jnp.exp(-gate)) * upper).astype(BF16)

    block = EXPERTS * CAP

    def down(chip):
        def one(s, carry):
            o = jnp.dot(active[...], wide[s], preferred_element_type=F32).astype(BF16)
            for owner in range(2):
                for half in range(2):
                    start = (owner * 4 + chip) * block + (s * 2 + half) * CAP
                    work[rows_at(start, CAP), :] = o[
                        owner * CAP : owner * CAP + CAP, half * UNIT : half * UNIT + UNIT
                    ]
            return carry

        lax.fori_loop(0, 8, one, 0)
        return links.copy(
            work.at[rows_at(((1 - core) * 4 + chip) * block, block)],
            partner.at[rows_at(chip * block, block)],
            other_core(),
        )

    def join(chip, made):
        made.wait_recv()
        add_into(
            work.at[rows_at((core * 4 + chip) * block, block)],
            partner.at[rows_at(chip * block, block)],
        )

    pair_own.wait_recv()
    gate_and_up(y)
    sum_own = down(y)
    from_below, from_above, from_far = below * 2 + core, above * 2 + core, far * 2 + core
    up_low.wait_recv()
    on_up = spread(from_below, low, along("y", 1))
    pair = [spread(from_below, low, other_core())]
    down_high.wait_recv()
    on_down = spread(from_above, high, along("y", -1))
    pair.append(spread(from_above, high, other_core()))
    join(y, sum_own)
    up_high.wait_recv()
    pair.append(spread(from_below, high, other_core()))
    down_low.wait_recv()
    pair.append(spread(from_above, low, other_core()))
    for made in pair:
        made.wait_recv()
    gate_and_up(above)
    sum_above = down(above)
    gate_and_up(below)
    on_up.wait_recv()
    pair_far = [spread(from_far, low, other_core())]
    on_down.wait_recv()
    pair_far.append(spread(from_far, high, other_core()))
    sum_below = down(below)
    ring_y = RingSum(links, "y", work, core * (4 * block), block, first_y, second_y)
    join(above, sum_above)
    join(below, sum_below)
    ring_y.direct()
    for made in pair_far:
        made.wait_recv()
    gate_and_up(far)
    sum_far = down(far)
    join(far, sum_far)
    ring_y.opposite()
    ring_y.relay()
    ring_y.arrived()

    back_moves = []
    for step in range(EXPERTS):
        to = (me + step) % EXPERTS
        total = ring_y.total(to * CAP, CAP).astype(BF16).astype(F32)
        piece = pl.ds(step * CAP, CAP)
        if step == 0:
            back[rows_at(me * CAP, CAP), :] = (total * share).astype(BF16)
            continue
        pieces[piece, :] = (total * share).astype(BF16)
        back_moves.append(
            links.copy(pieces.at[piece], back.at[rows_at(me * CAP, CAP)], exp_peer(step))
        )
    for made in back_moves:
        made.wait_recv()
    first = (((0,), (0,)), ((), ()))
    summed = lax.dot_general(table[...], back[...], first, preferred_element_type=F32)
    mixed[...] = (hidden[...].astype(F32) + summed).astype(BF16)

    out_moves = []
    for step in range(1, EXPERTS):
        to = (me + step) % EXPERTS
        out_moves.append(
            links.copy(
                mixed.at[rows_at(to * 32, 32)],
                rows_out.at[:, columns(me * UNIT, UNIT)],
                exp_peer(step),
            )
        )
    rows_out[:, columns(me * UNIT, UNIT)] = mixed[rows_at(me * 32, 32), :]
    for made in out_moves:
        made.wait_recv()
    out_ref[...] = rows_out[...]
    links.drain()


def layer(attn_out, out_full, residual, ids, gain, router, gate, up, down):
    vmem = pl.BlockSpec(memory_space=pltpu.VMEM)
    hbm = pl.BlockSpec(memory_space=pl.ANY)

    def rows(n, width=UNIT):
        return pltpu.VMEM((n, width), BF16)

    block = EXPERTS * CAP
    return pl.pallas_call(
        layer_kernel,
        out_shape=jax.ShapeDtypeStruct((32, 6144), BF16),
        in_specs=[vmem, hbm, vmem, vmem, vmem, vmem, hbm, hbm, hbm],
        out_specs=vmem,
        scratch_shapes=[
            pltpu.VMEM((8, 576, 768), BF16),
            rows(1152, 6144),
            rows(8 * block),
            rows(1024),
            rows(1024),
            rows(2048),
            rows(2048),
            rows(1024),
            rows(1024),
            rows(256),
            rows(256),
            rows(512),
            rows(512),
            rows(512),
            rows(512),
            rows(block, 512),
            rows(block),
            rows(CAP, 6144),
            rows(8 * CAP, 6144),
            rows(2 * CAP, 576),
            rows(4 * block),
            rows(block),
            rows(2 * block),
            rows(block),
            rows(512),
            rows(32, 6144),
            pltpu.SemaphoreType.DMA((11,)),
            pltpu.SemaphoreType.DMA((LINKS,)),
            pltpu.SemaphoreType.DMA((LINKS,)),
        ],
        compiler_params=pltpu.CompilerParams(
            collective_id=0, has_side_effects=True, vmem_limit_bytes=62 << 20
        ),
        name="layer",
    )(attn_out, out_full, residual, ids, gain, router, gate, up, down)


def prefix(array, axis, join, neutral):
    place = lax.axis_index(axis)
    gathered = jax.tree.map(
        lambda a, kind: lax.all_gather(a.astype(kind), axis), array, (jnp.bfloat16, jnp.bfloat16)
    )
    state = jax.tree.map(lambda a, e: jnp.zeros_like(a) + jnp.asarray(e, a.dtype), array, neutral)

    def one(lap, state):
        return join(
            state,
            jax.tree.map(
                lambda a, own: lax.dynamic_index_in_dim(a, lap, 0, False).astype(own.dtype),
                gathered,
                array,
            ),
        )

    return lax.fori_loop(0, place, one, state)


def head_norm(values, gain):
    squares = jnp.mean(values * values, axis=-1, keepdims=True)
    scaled = values * lax.rsqrt(squares + 1e-06) * gain.reshape(1, values.shape[1], -1)
    return scaled.astype(jnp.bfloat16).reshape(values.shape[0], -1)


def chain_step(earlier, later):
    return (earlier[0] + later[0], jnp.exp(later[0])[:, None, None] * earlier[1] + later[1])


def per_device(
    query_rows,
    key_rows,
    value_rows,
    log_decay,
    attn_gain,
    out_weight,
    residual,
    ffn_gain,
    router,
    expert_ids,
    w_gate,
    w_up,
    w_down,
):
    length = query_rows.shape[0]
    heads = log_decay.shape[1]
    queries = query_rows.reshape(length, heads, -1)
    keys_all = key_rows.reshape(length, heads, -1)
    values_all = value_rows.reshape(length, heads, -1)
    running = jnp.cumsum(log_decay, axis=0)
    later_pos = lax.broadcasted_iota(jnp.int32, (length, length), 0)
    earlier_pos = lax.broadcasted_iota(jnp.int32, (length, length), 1)
    spread = jnp.transpose(running)[:, :, None] - jnp.transpose(running)[:, None, :]
    decay = jnp.where((later_pos >= earlier_pos)[None], jnp.exp(jnp.minimum(spread, 0.0)), 0.0)
    scores = jnp.einsum("thd,shd->hts", queries, keys_all, preferred_element_type=jnp.float32)
    weights = (scores * decay).astype(jnp.bfloat16)
    inner = jnp.einsum("hts,shd->thd", weights, values_all, preferred_element_type=jnp.float32)
    to_end = jnp.exp(running[-1][None, :] - running)
    decayed_keys = (keys_all.astype(jnp.float32) * to_end[:, :, None]).astype(jnp.bfloat16)
    own_state = jnp.einsum(
        "shd,she->hde", decayed_keys, values_all, preferred_element_type=jnp.float32
    )
    block_decay = running[-1]
    identity = (jnp.zeros_like(block_decay), jnp.zeros_like(own_state))
    carried = prefix((block_decay, own_state), "ctx", chain_step, identity)[1]
    scaled_query = queries.astype(jnp.float32) * jnp.exp(running)[:, :, None]
    cross = jnp.einsum("thd,hde->the", scaled_query, carried, precision=lax.Precision.HIGHEST)
    attn_out = head_norm(inner + cross, attn_gain)
    out_full = lax.all_gather(out_weight, "ctx", axis=0)
    return layer(
        attn_out,
        out_full,
        residual,
        expert_ids.T,
        ffn_gain.reshape(1, -1),
        router.T,
        w_gate[0].T,
        w_up[0].T,
        w_down[0],
    )


def solution(mesh):
    return jax.shard_map(
        per_device,
        mesh=mesh,
        in_specs=(
            P("ctx", "exp"),
            P("ctx", "exp"),
            P("ctx", "exp"),
            P("ctx", "exp"),
            P("exp"),
            P("exp", "ctx"),
            P(("ctx", "exp"), None),
            P(),
            P(),
            P("ctx", None),
            P("exp", None, "ctx"),
            P("exp", None, "ctx"),
            P("exp", "ctx", None),
        ),
        out_specs=P(("ctx", "exp"), None),
        check_vma=False,
    )
```

time: 464 us -> 262 us (0.56)
  waiting for transfers between devices: 365 us -> 51.5 us
  Pallas kernels: 0 us -> 172 us
  matrix products: 62.3 us -> 6.44 us
  other arithmetic: 7.34 us -> 1.78 us
    reduce_scatter x3 -> x0, waiting for transfers between devices: 205 us -> none  [the longest x1 81.8 us: per_device(): lax.psum_scatter(jnp.dot(attn_out, out_full, preferred_element_type=jnp.f...]
    pallas_call x0 -> x1, Pallas kernels: none -> 172 us  [layer(): pl.pallas_call(layer_kernel, out_shape=jax.ShapeDtypeStruct((32, 6144), B...]
    all_gather x3 -> x1, waiting for transfers between devices: 148 us -> 39.8 us  [per_device(): out_full = lax.all_gather(out_weight, 'ctx', axis=0)]
    dot_general x7 -> x0, matrix products: 55.8 us -> none  [the longest x1 10.9 us: per_device(): gate = jnp.dot(piece, gate_cols, preferred_element_type=jnp.float32)]
  transfers between devices with their start and end apart: 7 -> 2, of which waited for: 7 -> 2; matrix products, arithmetic and copies ran while one was open for 3% -> 2% of each run, Pallas kernels for 0% -> 0%
where the time goes in v1:
time: 262 us
  Pallas kernels  172 us (66%)
  waiting for transfers between devices  51.5 us (20%)
  between operations  13.5 us (5%)
  blocking collectives  10.8 us (4%)
  matrix products  6.44 us (2%)
  local copies, waits for them, and re-layouts  5.58 us (2%)
    pallas_call x1, Pallas kernels, layer(): pl.pallas_call(layer_kernel, out_shape=jax.ShapeDtypeStruct((32, 6144), B...  172 us
    all_gather x1, waiting for transfers between devices, per_device(): out_full = lax.all_gather(out_weight, 'ctx', axis=0)  39.8 us
    all_gather x1, waiting for transfers between devices, prefix(): lax.all_gather(a.astype(kind), axis)  10.9 us
    all_gather x1, blocking collectives, prefix(): lax.all_gather(a.astype(kind), axis)  10.8 us
  transfers between devices with their start and end apart: 2, of which 2 were waited for; matrix products, arithmetic and copies ran while one was open for 2% of the time, Pallas kernels for 0%

profile of v1, /device:TPU:0, one launch (start us, length us, event | category | flops | bytes accessed | tf_op | source)
XLA Modules:
  0.0 261.8 jit_solution(3333826799903002808)
XLA Ops:
  6.5 0.0 copy-start
  6.5 0.0 all-gather.6.cloned.1.call-start
  6.5 0.8 reshape.77
  7.3 1.2 reduce-window.6
  8.5 0.2 slice_reduce_fusion
  8.7 0.2 reduce-window.9
  8.9 0.1 add_bitcast_fusion
  8.9 0.2 slice_reduce_fusion.1
  9.1 0.1 bitcast_exponential_fusion
  9.2 1.3 copy.71
  10.5 2.0 convolution_convert_fusion
  12.5 0.0 all-gather.6.cloned.1.call-update
  12.5 0.0 all-gather.8.cloned.1.call-start
  12.5 0.7 all-gather.8.cloned.1.call-update
  13.2 0.2 fusion.17
  13.4 10.8 %all-gather.2 = bf16[8,1,4]{2,1,0:T(2,128)(2,1)S(1)} all-gather(bf16[1,1,4]{2,1,0:T(2,128)(2,1)S(1)} %bitcast.100), channel_id=1, replica_groups=mesh['ctx'=8,'exp'=16] {'ctx'}, dimensions={0}, use_global_device_ids=true | all-gather | bytes 72 | tf_op jit(solution)/shard_map/all_gather | solution.py:545
  24.3 0.1 copy.62
  24.4 0.1 copy.65
  24.5 0.1 iota_compare_fusion
  24.5 0.0 copy-done
  24.5 3.0 %fusion.1 = f32[512,4,128]{0,2,1:T(8,128)S(1)} fusion(bf16[512,4,128]{0,2,1:T(8,128)(2,1)S(1)} %bitcast.88, f32[4,512]{1,0:T(4,128)S(1)} %bitcast.94, pred[512,512]{1,0:T(8,128)(4,1)S(1)} %iota_compare_fusion, bf16[512,512]{1,0:T(8,128)(2,1)} %param.17, bf16[512,512]{1,0:T(8,128)(2,1)S(1)} %copy-done), kind=kOutput, calls=%fused_computation.4 | convolution fusion | flops 542113792 | bytes 2891776 | tf_op jit(solution)/shard_map/hts,shd->thd/dot_general | solution.py:599
  27.6 0.0 copy-start.1
  27.6 10.9 %all-gather.6.cloned.1.call-done = bf16[32,128,128]{2,1,0:T(8,128)(2,1)} async-done(((bf16[4,128,128]{2,1,0:T(8,128)(2,1)}), bf16[32,128,128]{2,1,0:T(8,128)(2,1)}) %all-gather.6.cloned.1.call-update) | async-done | bytes 1048592 | tf_op jit(solution)/shard_map/all_gather | solution.py:545
  38.6 1.4 multiply_reduce_fusion
  40.0 0.0 copy-done.1
  40.0 0.2 multiply_convert_fusion.1
  40.2 1.0 copy.70.attn_ref
  41.2 39.8 %all-gather.8.cloned.1.call-done = bf16[4096,768]{1,0:T(8,128)(2,1)} async-done(((bf16[512,768]{1,0:T(8,128)(2,1)}), bf16[4096,768]{1,0:T(8,128)(2,1)}) %all-gather.8.cloned.1.call-update) | async-done | bytes 6291472 | tf_op jit(solution)/shard_map/all_gather | solution.py:611
  81.0 172.1 %layer.1 = bf16[32,6144]{1,0:T(8,128)(2,1)} custom-call(bf16[512,512]{1,0:T(8,128)(2,1)} %copy.70.attn_ref, bf16[8,512,768]{2,1,0:T(8,128)(2,1)} %bitcast.85, bf16[32,6144]{1,0:T(8,128)(2,1)} %resid_ref.1, s32[2,512]{1,0:T(2,128)} %bitcast.97, f32[1,6144]{1,0:T(1,128)} %bitcast.91, f32[16,6144]{1,0:T(8,128)} %bitcast.90, bf16[576,6144]{1,0:T(8,128)(2,1)} %bitcast.82, ...), custom_call_target="tpu_custom_call" | custom-call | tf_op jit(solution)/shard_map/layer/pallas_call | solution.py:499
  253.2 1.8 copy.109
  (4 shorter events, 0.0 us)
Async XLA Ops:
  6.5 18.0 %copy-start = (bf16[512,512]{1,0:T(8,128)(2,1)S(1)}, bf16[512,512]{1,0:T(8,128)(2,1)}, u32[]{:S(2)}) copy-start(bf16[512,512]{1,0:T(8,128)(2,1)} %param.15) | copy-start | bytes 1572868
  6.5 32.0 %all-gather.6.cloned.1.call-start = ((), (), s32[]{:S(2)}) async-start(), calls=%async_computation | async-start | bytes 1179648 | tf_op jit(solution)/shard_map/all_gather | solution.py:545
  12.5 68.5 %all-gather.8.cloned.1.call-start = ((), (), s32[]{:S(2)}) async-start(), calls=%async_computation.1 | async-start | bytes 7077888 | tf_op jit(solution)/shard_map/all_gather | solution.py:611
  27.6 12.4 %copy-start.1 = (f32[512]{0:T(512)S(1)}, f32[512]{0:T(512)}, u32[]{:S(2)}) copy-start(f32[512]{0:T(512)} %param.19) | copy-start | bytes 6148
Sparse Core Ops, SparseCore 0:
  12.6 25.8 all-gather.5
  40.2 40.7 all-gather.7

commit v2 on v0

v2 whole, which is shorter than its diff:
```python
import functools

import jax
import jax.numpy as jnp
from jax import lax
from jax.experimental import pallas as pl
from jax.experimental.pallas import tpu as pltpu
from jax.sharding import PartitionSpec as P

MESH = pl.DeviceIdType.MESH
F32 = jnp.float32
BF16 = jnp.bfloat16
EXPERTS = 16
CAP = 80
UNIT = 128
STAGES = 3
LINKS = 288


def place():
    ctx = lax.axis_index("ctx")
    exp = lax.axis_index("exp")
    return ctx // 2, ctx % 2, exp // 4, exp % 4


def along(axis, step):
    y, core, x, z = place()
    step = step % 4
    if axis == "x":
        return (y * 2 + core, (x + step) % 4 * 4 + z)
    if axis == "z":
        return (y * 2 + core, x * 4 + (z + step) % 4)
    return ((y + step) % 4 * 2 + core, x * 4 + z)


def exp_peer(step):
    return (lax.axis_index("ctx"), (lax.axis_index("exp") + step) % EXPERTS)


def ctx_peer(step):
    return ((lax.axis_index("ctx") + step) % 8, lax.axis_index("exp"))


def other_core():
    y, core, _, _ = place()
    return (y * 2 + 1 - core, lax.axis_index("exp"))


class Links:
    def __init__(self, send, recv):
        self.send, self.recv, self.count = send, recv, 0
        self.open, self.done = [], 0

    def copy(self, src, dst, device):
        made = pltpu.make_async_remote_copy(
            src_ref=src,
            dst_ref=dst,
            send_sem=self.send.at[self.count],
            recv_sem=self.recv.at[self.count],
            device_id=device,
            device_id_type=MESH,
        )
        made.start()
        self.count += 1
        assert self.count <= LINKS
        self.open.append(made)
        return made

    def drain(self, until=None):
        until = self.count if until is None else until
        for made in self.open[self.done : until]:
            made.wait_send()
        self.done = max(self.done, until)


def add_into(target, extra):
    size = 128 if target.shape[0] % 128 == 0 else 80

    def one(i, carry):
        rows = rows_at(i * size, size)
        target[rows, :] = (target[rows, :].astype(F32) + extra[rows, :].astype(F32)).astype(BF16)
        return carry

    lax.fori_loop(0, target.shape[0] // size, one, 0)


class RingSum:
    def __init__(self, links, axis, part, base, n, stride, first, second):
        place_of = dict(zip(("y", "core", "x", "z"), place()))
        self.links, self.axis, self.i = links, axis, place_of[axis]
        self.part, self.base, self.n, self.stride = part, base, n, stride
        self.first, self.second = first, second

    def low(self, d):
        return self.part.at[rows_at(self.base + d * self.stride, self.n // 2)]

    def high(self, d):
        return self.part.at[rows_at(self.base + d * self.stride + self.n // 2, self.n // 2)]

    def slot(self, k):
        return pl.ds(k * (self.n // 2), self.n // 2)

    def opposite(self):
        far, slot = (self.i + 2) % 4, self.slot
        up = self.links.copy(self.low(far), self.first.at[slot(0)], along(self.axis, 1))
        down = self.links.copy(self.high(far), self.first.at[slot(1)], along(self.axis, -1))
        self.far = (up, down)

    def direct_up(self):
        up, slot = (self.i + 1) % 4, self.slot
        self.near = [self.links.copy(self.high(up), self.second.at[slot(1)], along(self.axis, 1))]

    def direct_down(self):
        down, slot = (self.i + 3) % 4, self.slot
        self.near.append(
            self.links.copy(self.low(down), self.second.at[slot(2)], along(self.axis, -1))
        )

    def relay(self):
        up, down, slot = (self.i + 1) % 4, (self.i + 3) % 4, self.slot
        self.far[0].wait_recv()
        add_into(self.low(up), self.first.at[slot(0)])
        self.near.append(
            self.links.copy(self.low(up), self.second.at[slot(0)], along(self.axis, 1))
        )
        self.far[1].wait_recv()
        add_into(self.high(down), self.first.at[slot(1)])
        self.near.append(
            self.links.copy(self.high(down), self.second.at[slot(3)], along(self.axis, -1))
        )

    def arrived(self):
        for made in self.near:
            made.wait_recv()

    def total(self, start, size):
        own = self.part[rows_at(self.base + self.i * self.stride + start, size), :].astype(F32)
        own = own + self.second[rows_at(start, size), :].astype(F32)
        return own + self.second[rows_at(self.n + start, size), :].astype(F32)


def columns(start, size):
    return pl.ds(pl.multiple_of(start, 128), size)


def rows_at(start, size):
    return pl.ds(pl.multiple_of(start, 16), size)


def split3(value):
    one = value.astype(BF16)
    rest = value - one.astype(F32)
    two = rest.astype(BF16)
    return one, two, (rest - two.astype(F32)).astype(BF16)


def layer_kernel(
    query_ref,
    key_ref,
    value_ref,
    decay_ref,
    head_gain_ref,
    out_w_ref,
    resid_ref,
    ids_ref,
    gain_ref,
    router_ref,
    gate_ref,
    up_ref,
    down_ref,
    out_ref,
    state,
    chip_state,
    states,
    carried,
    gone,
    attn_ref,
    wide,
    gate_up,
    work,
    second,
    half,
    last_first,
    last_second,
    resid_parts,
    resid_cols,
    hidden,
    table,
    pieces,
    rows_in,
    tokens,
    scales,
    sums,
    active,
    partner,
    first_y,
    second_y,
    back,
    rows_out,
    local,
    send,
    recv,
    state_send,
    state_recv,
):
    y, core, x, z = place()
    ctx = y * 2 + core
    me = lax.axis_index("exp")
    links = Links(send, recv)
    above, below, far = (y + 1) % 4, (y + 3) % 4, (y + 2) % 4

    def chip_at(home, k):
        return (home + (0, 1, 3, 2)[k]) % 4

    def unit_cols(j):
        k = j // 12
        chip = (y + k + k // 2 - 2 * (k // 3)) % 4
        return columns(chip * 1536 + j % 12 * UNIT, UNIT)

    load_gate = pltpu.make_async_copy(gate_ref, gate_up.at[pl.ds(0, 576)], local.at[1])
    load_up = pltpu.make_async_copy(up_ref, gate_up.at[pl.ds(576, 576)], local.at[2])
    w_all, w_low, w_high = pl.ds(0, 512), pl.ds(0, 256), pl.ds(256, 256)

    def w_part(chip, side, rows):
        return wide.at[chip, rows, columns(side * 768, 768)]

    load_w = pltpu.make_async_copy(out_w_ref, w_part(y, core, w_all), local.at[0])
    load_w.start()

    barrier = pltpu.get_barrier_semaphore()
    for device in [along("y", 1), along("y", 3), other_core(), along("y", 2)]:
        pl.semaphore_signal(barrier, inc=1, device_id=device, device_id_type=MESH)
    for step in range(1, EXPERTS):
        pl.semaphore_signal(barrier, inc=1, device_id=exp_peer(step), device_id_type=MESH)

    earlier = lax.broadcasted_iota(jnp.int32, (512, 512), 1) <= lax.broadcasted_iota(
        jnp.int32, (512, 512), 0
    )
    lower = jnp.where(earlier, 1.0, 0.0).astype(BF16)
    turned = (((1,), (1,)), ((), ()))
    first = (((0,), (0,)), ((), ()))
    run_col = jnp.zeros((512, 4), F32)
    run_row = jnp.zeros((4, 512), F32)
    for term in split3(decay_ref[...]):
        run_col = run_col + lax.dot_general(lower, term, turned, preferred_element_type=F32)
        run_row = run_row + lax.dot_general(term, lower, turned, preferred_element_type=F32)
    lines = lax.broadcasted_iota(jnp.int32, (4, 128), 0)
    ends = jnp.zeros((4, 128), F32)
    for h in range(4):
        lanes = pl.ds(h * 128, 128)
        end = run_col[511:512, h : h + 1]
        to_end = jnp.exp(end - run_col[:, h : h + 1])
        decayed = (key_ref[:, lanes].astype(F32) * to_end).astype(BF16)
        own = lax.dot_general(decayed, value_ref[:, lanes], first, preferred_element_type=F32)
        state[pl.ds(h * 128, 128), :] = own.astype(BF16)
        ends = jnp.where(lines == h, end, ends)

    def pack_ends(value):
        parts = [t.astype(F32) for t in split3(value)]
        return jnp.concatenate(parts + [jnp.zeros((4, 128), F32)], axis=0).astype(BF16)

    def ends_of(ref):
        value = ref[pl.ds(512, 16), :].astype(F32)
        return value[0:4] + value[4:8] + value[8:12]

    state[pl.ds(512, 16), :] = pack_ends(ends)

    pl.semaphore_wait(barrier, EXPERTS + 3)

    def state_copy(src, dst, k, device):
        return pltpu.make_async_remote_copy(
            src_ref=src,
            dst_ref=dst,
            send_sem=state_send.at[k],
            recv_sem=state_recv.at[k],
            device_id=device,
            device_id_type=MESH,
        )

    def state_pair():
        return state_copy(state, states.at[0], 0, other_core())

    def state_up(step):
        return state_copy(chip_state, states.at[step], step, along("y", step))

    def state_over(step):
        return state_copy(states.at[step], states.at[step], 4 + step, other_core())

    @pl.when(core == 0)
    def _():
        state_pair().start()

    def spread_w(chip, side, rows, device, own=False):
        return links.copy(out_w_ref.at[rows] if own else w_part(chip, side, rows), w_part(chip, side, rows), device)

    w_up_low = spread_w(y, core, w_low, along("y", 1), True)
    w_down_high = spread_w(y, core, w_high, along("y", -1), True)
    w_pair = [spread_w(y, core, w_all, other_core(), True)]

    @pl.when(core == 1)
    def _():
        state_pair().wait_recv()
        own_ends = ends_of(state)
        for h in range(4):
            rows = pl.ds(h * 128, 128)
            joined = jnp.exp(own_ends[h : h + 1]) * states[0, rows, :].astype(F32)
            chip_state[rows, :] = (joined + state[rows, :].astype(F32)).astype(BF16)
        chip_state[pl.ds(512, 16), :] = pack_ends(own_ends + ends_of(states.at[0]))
        for step in range(1, 4):

            @pl.when(y + step < 4)
            def _(step=step):
                state_up(step).start()

    w_up_high = spread_w(y, core, w_high, along("y", 1), True)
    w_down_low = spread_w(y, core, w_low, along("y", -1), True)
    load_gate.start()
    load_up.start()

    def resid_part(g, carry):
        for s in range(STAGES):
            resid_parts[g, :, pl.ds(s * UNIT, UNIT)] = resid_ref[:, unit_cols(s * EXPERTS + g)]
        return carry

    lax.fori_loop(0, EXPERTS, resid_part, 0)
    resid_moves = []
    for step in range(1, EXPERTS):
        to = (me + step) % EXPERTS
        resid_moves.append(
            links.copy(resid_parts.at[to], resid_cols.at[rows_at(me * 32, 32)], exp_peer(step))
        )
    resid_cols[rows_at(me * 32, 32), :] = resid_parts[me]

    for h in range(4):
        lanes = pl.ds(h * 128, 128)
        for r in range(2):
            seen = (r + 1) * 256
            rows = pl.ds(r * 256, 256)
            scores = lax.dot_general(
                query_ref[rows, lanes],
                key_ref[pl.ds(0, seen), lanes],
                turned,
                preferred_element_type=F32,
            )
            spread_of = run_col[r * 256 : seen, h : h + 1] - run_row[h : h + 1, :seen]
            late = lax.broadcasted_iota(jnp.int32, (256, seen), 0) + r * 256
            soon = lax.broadcasted_iota(jnp.int32, (256, seen), 1)
            decay = jnp.where(late >= soon, jnp.exp(jnp.minimum(spread_of, 0.0)), 0.0)
            sums[rows, lanes] = jnp.dot(
                (scores * decay).astype(BF16),
                value_ref[pl.ds(0, seen), lanes],
                preferred_element_type=F32,
            )

    for step in range(1, 4):

        @pl.when((core == 1) & (y >= step))
        def _(step=step):
            state_up(step).wait_recv()
            state_over(step).start()

    w_up_low.wait_recv()
    w_on_up = spread_w(below, core, w_low, along("y", 1))
    w_pair.append(spread_w(below, core, w_low, other_core()))
    w_down_high.wait_recv()
    w_on_down = spread_w(above, core, w_high, along("y", -1))
    w_pair.append(spread_w(above, core, w_high, other_core()))

    experts = lax.broadcasted_iota(jnp.int32, (EXPERTS, 512), 0)
    picked = (ids_ref[0:1, :] == experts) | (ids_ref[1:2, :] == experts)
    before = lax.broadcasted_iota(jnp.int32, (512, 512), 0) < lax.broadcasted_iota(
        jnp.int32, (512, 512), 1
    )
    rank = jnp.dot(
        jnp.where(picked, 1.0, 0.0).astype(BF16),
        jnp.where(before, 1.0, 0.0).astype(BF16),
        preferred_element_type=F32,
    )
    code = jnp.where(picked, rank, -1.0)
    slots = lax.broadcasted_iota(jnp.int32, (CAP, 512), 0).astype(F32)
    for e in range(EXPERTS):
        table[pl.ds(e * CAP, CAP), :] = jnp.where(code[e : e + 1, :] == slots, 1.0, 0.0).astype(
            BF16
        )

    carried[...] = jnp.zeros((512, 128), F32)
    gone[...] = jnp.zeros((4, 128), F32)
    for step in range(1, 4):

        @pl.when((core == 0) & (y >= step))
        def _(step=step):
            state_over(step).wait_recv()

        @pl.when(y >= step)
        def _(step=step):
            for h in range(4):
                rows = pl.ds(h * 128, 128)
                kept = jnp.exp(gone[pl.ds(h, 1), :])
                carried[rows, :] = carried[rows, :] + kept * states[step, rows, :].astype(F32)
            gone[...] = gone[...] + ends_of(states.at[step])

    @pl.when(core == 1)
    def _():
        pair_ends = ends_of(states.at[0])
        for h in range(4):
            rows = pl.ds(h * 128, 128)
            kept = jnp.exp(pair_ends[h : h + 1])
            carried[rows, :] = kept * carried[rows, :] + states[0, rows, :].astype(F32)

    for h in range(4):
        lanes = pl.ds(h * 128, 128)
        full = carried[lanes, :]
        near = full.astype(BF16)
        rest = (full - near.astype(F32)).astype(BF16)
        asked = query_ref[:, lanes]
        cross = jnp.dot(asked, near, preferred_element_type=F32)
        cross = cross + jnp.dot(asked, rest, preferred_element_type=F32)
        total = sums[pl.ds(0, 512), lanes] + jnp.exp(run_col[:, h : h + 1]) * cross
        mean = jnp.mean(total * total, axis=1, keepdims=True)
        attn_ref[:, lanes] = (
            total * lax.rsqrt(mean + 1e-06) * head_gain_ref[:, lanes]
        ).astype(BF16)

    w_up_high.wait_recv()
    w_pair.append(spread_w(below, core, w_high, other_core()))
    w_down_low.wait_recv()
    w_pair.append(spread_w(above, core, w_low, other_core()))
    load_w.wait()
    for made in w_pair:
        made.wait_recv()

    rings_a, rings_b, lasts_a, lasts_b = [], [], [], []
    for s in range(STAGES):
        for which, (rings, axis) in enumerate(((rings_a, "x"), (rings_b, "z"))):
            k = which * STAGES + s
            rings.append(
                RingSum(
                    links,
                    axis,
                    work,
                    k * 4096,
                    1024,
                    1024,
                    work.at[pl.ds(6 * 4096 + k * 1024, 1024)],
                    second.at[pl.ds(k * 2048, 2048)],
                )
            )
        for which, (rings, axis) in enumerate(((lasts_a, "z"), (lasts_b, "x"))):
            k = which * STAGES + s
            rings.append(
                RingSum(
                    links,
                    axis,
                    half,
                    k * 1024,
                    256,
                    256,
                    last_first.at[pl.ds(k * 256, 256)],
                    last_second.at[pl.ds(k * 512, 512)],
                )
            )

    def project_quad(s, to):
        quad = s * 4 + to
        k = quad // 3
        chip = (y + k + k // 2 - 2 * (k // 3)) % 4
        w = wide[chip, pl.ds(0, 512), columns(quad % 3 * 512, 512)]
        r = jnp.dot(attn_ref[...], w, preferred_element_type=F32).astype(BF16)
        for u in range(4):
            for side in range(2):
                start = s * 4096 + to * 1024 + (side * 4 + u) * 128
                work[rows_at(start, 128), :] = r[
                    side * 128 : side * 128 + 128, u * UNIT : u * UNIT + UNIT
                ]
                start = (STAGES + s) * 4096 + u * 1024 + (side * 4 + to) * 128
                work[rows_at(start, 128), :] = r[
                    256 + side * 128 : 256 + side * 128 + 128, u * UNIT : u * UNIT + UNIT
                ]

    def project(s):
        def one(i, carry):
            project_quad(s, (x + 3 + i) % 4)
            return carry

        project_quad(s, (x + 2) % 4)
        rings_a[s].opposite()
        lax.fori_loop(0, 3, one, 0)
        rings_b[s].opposite()
        rings_a[s].direct_up()
        rings_a[s].direct_down()
        rings_b[s].direct_up()
        rings_b[s].direct_down()

    def relay(s):
        rings_a[s].relay()
        rings_b[s].relay()

    def turn(s):
        for ring, last in ((rings_a[s], lasts_a[s]), (rings_b[s], lasts_b[s])):
            ring.arrived()

            def one(u, carry, ring=ring, last=last):
                for side in range(2):
                    rows = rows_at(last.base + u * 256 + side * 128, 128)
                    half[rows, :] = ring.total(side * 512 + u * 128, 128).astype(BF16)
                return carry

            lax.fori_loop(0, 4, one, 0)
            last.opposite()
            last.direct_up()
            last.direct_down()

    def turn_relay(s):
        lasts_a[s].relay()
        lasts_b[s].relay()

    row_moves = [[] for _ in range(STAGES)]

    def dispatch(s):
        cols = pl.ds(s * UNIT, UNIT)
        if s == 0:
            for made in resid_moves:
                made.wait_recv()
        for start, ring in ((0, lasts_a[s]), (256, lasts_b[s])):
            ring.arrived()
            rows = pl.ds(start, 256)
            hidden[rows, cols] = (
                ring.total(0, 256) + resid_cols[rows, cols].astype(F32)
            ).astype(BF16)
        found = jnp.dot(table[...], hidden[:, cols], preferred_element_type=F32)
        pieces[pl.ds(s * EXPERTS * CAP, EXPERTS * CAP), :] = found.astype(BF16)
        lands = rows_in.at[:, columns((s * EXPERTS + me) * UNIT, UNIT)]
        for step in range(1, EXPERTS):
            to = (me + step) % EXPERTS
            piece = pieces.at[rows_at((s * EXPERTS + to) * CAP, CAP)]
            row_moves[s].append(links.copy(piece, lands, exp_peer(step)))
        lands[...] = pieces[rows_at((s * EXPERTS + me) * CAP, CAP), :]

    squares = [jnp.zeros((CAP, 1), F32)]
    mine = rows_at(ctx * CAP, CAP)
    gathers = [None] * STAGES

    def spread(s, block, side, device):
        cols = pl.ds(s * 2048 + side * 1024, 1024)
        if side == 2:
            cols = pl.ds(s * 2048, 2048)
        ref = tokens.at[rows_at(block * CAP, CAP), cols]
        return links.copy(ref, ref, device)

    def gather(s):
        for made in row_moves[s]:
            made.wait_recv()
        for u in range(EXPERTS):
            cols = pl.ds((s * EXPERTS + u) * UNIT, UNIT)
            part = rows_in[:, cols].astype(F32)
            squares[0] = squares[0] + jnp.sum(part * part, axis=1, keepdims=True)
            tokens[mine, cols] = (part * gain_ref[:, unit_cols(s * EXPERTS + u)]).astype(BF16)
        gathers[s] = dict(
            up_low=spread(s, ctx, 0, along("y", 1)),
            down_high=spread(s, ctx, 1, along("y", -1)),
            up_high=spread(s, ctx, 1, along("y", 1)),
            down_low=spread(s, ctx, 0, along("y", -1)),
            pair=[spread(s, ctx, 2, other_core())],
        )

    from_below, from_above, from_far = below * 2 + core, above * 2 + core, far * 2 + core

    def gather_mid(s):
        g = gathers[s]
        g["up_low"].wait_recv()
        g["on_up"] = spread(s, from_below, 0, along("y", 1))
        g["near"] = [spread(s, from_below, 0, other_core())]
        g["down_high"].wait_recv()
        g["on_down"] = spread(s, from_above, 1, along("y", -1))
        g["near"].append(spread(s, from_above, 1, other_core()))

    def gather_near(s):
        g = gathers[s]
        g["up_high"].wait_recv()
        g["near"].append(spread(s, from_below, 1, other_core()))
        g["down_low"].wait_recv()
        g["near"].append(spread(s, from_above, 0, other_core()))

    def gather_far(s):
        g = gathers[s]
        g["on_up"].wait_recv()
        g["far"] = [spread(s, from_far, 0, other_core())]
        g["on_down"].wait_recv()
        g["far"].append(spread(s, from_far, 1, other_core()))

    def held(s, names):
        for name in names:
            for made in gathers[s][name]:
                made.wait_recv()

    def gate_and_up(s, chip):
        rows = rows_at(chip * (2 * CAP), 2 * CAP)
        total = None
        quad = s * 4
        while quad < s * 4 + 4:
            run = min(3 - quad % 3, s * 4 + 4 - quad)
            start = columns(chip_at(chip, quad // 3) * 1536 + quad % 3 * 512, run * 512)
            part = lax.dot_general(
                tokens[rows, pl.ds(quad * 512, run * 512)],
                gate_up[:, start],
                turned,
                preferred_element_type=F32,
            )
            total = part if total is None else total + part
            quad += run
        if s > 0:
            total = total + sums[rows, :]
        if s < STAGES - 1:
            sums[rows, :] = total
            return
        total = total * scales[rows, 0:1]
        gate, upper = total[:, :576], total[:, 576:]
        active[...] = (gate / (1.0 + jnp.exp(-gate)) * upper).astype(BF16)

    def gate_and_up_all(s):
        def one(chip, carry):
            gate_and_up(s, chip)
            return carry

        lax.fori_loop(0, 4, one, 0)

    project(0)
    relay(0)
    project(1)
    turn(0)
    w_on_up.wait_recv()
    w_pair_far = [spread_w(far, core, w_low, other_core())]
    w_on_down.wait_recv()
    w_pair_far.append(spread_w(far, core, w_high, other_core()))
    relay(1)
    turn_relay(0)
    for made in w_pair_far:
        made.wait_recv()
    project(2)
    dispatch(0)
    turn(1)
    relay(2)
    turn_relay(1)
    gather(0)
    dispatch(1)
    turn(2)
    gather_mid(0)
    turn_relay(2)
    gather(1)
    gather_near(0)
    dispatch(2)
    sent_rows = links.count
    gather_far(0)
    gather_mid(1)
    links.drain(sent_rows)
    load_down = []
    for k in range(4):
        made = pltpu.make_async_copy(
            down_ref.at[:, pl.ds(k * 1536, 1536)], wide.at[k], local.at[3 + k]
        )
        made.start()
        load_down.append(made)
    load_gate.wait()
    load_up.wait()
    held(0, ("pair", "near", "far"))
    gather(2)

    def spread_scale(block, device):
        ref = scales.at[rows_at(block * CAP, CAP)]
        return links.copy(ref, ref, device)

    scale = lax.rsqrt(squares[0] / 6144.0 + 1e-05)
    scales[mine, :] = jnp.broadcast_to(scale, (CAP, UNIT))
    scale_up = spread_scale(ctx, along("y", 1))
    scale_down = spread_scale(ctx, along("y", -1))
    scale_pair = [spread_scale(ctx, other_core())]
    gather_near(1)
    gather_far(1)
    gate_and_up_all(0)
    gather_mid(2)
    scale_up.wait_recv()
    scale_on = spread_scale(from_below, along("y", 1))
    scale_pair.append(spread_scale(from_below, other_core()))
    scale_down.wait_recv()
    scale_pair.append(spread_scale(from_above, other_core()))
    held(1, ("pair", "near", "far"))
    gate_and_up_all(1)
    gather_near(2)
    scale_on.wait_recv()
    scale_pair.append(spread_scale(from_far, other_core()))

    my_ids = lax.dot_general(
        table[rows_at(me * CAP, CAP), :],
        ids_ref[...].astype(F32).astype(BF16),
        turned,
        preferred_element_type=F32,
    )
    logits = jnp.zeros((CAP, EXPERTS), F32)
    for k in range(4):
        part = router_ref[:, columns(chip_at(y, k) * 1536, 1536)]
        router_high = part.astype(BF16)
        router_low = (part - router_high.astype(F32)).astype(BF16)
        token = tokens[mine, pl.ds(k * 1536, 1536)]
        for w in (router_high, router_low):
            logits = logits + lax.dot_general(token, w, turned, preferred_element_type=F32)
    gates = 1.0 / (1.0 + jnp.exp(-logits * scale))
    lanes = lax.broadcasted_iota(jnp.int32, (CAP, EXPERTS), 1)
    lanes_f = lanes.astype(F32)
    both = (my_ids[:, 0:1] == lanes_f) | (my_ids[:, 1:2] == lanes_f)
    total = jnp.sum(jnp.where(both, gates, 0.0), axis=1, keepdims=True)
    share = jnp.sum(jnp.where(lanes == me, gates, 0.0), axis=1, keepdims=True) / total

    block = EXPERTS * CAP
    for made in load_down:
        made.wait()

    def down(chip):
        def one(quad, carry):
            k = quad // 3
            part = (chip + k + k // 2 - 2 * (k // 3)) % 4
            w = wide[part, :, columns(quad % 3 * 512, 512)]
            o = jnp.dot(active[...], w, preferred_element_type=F32).astype(BF16)
            for owner in range(2):
                for u in range(4):
                    start = (owner * 4 + chip) * (STAGES * block) + (quad * 4 + u) * CAP
                    work[rows_at(start, CAP), :] = o[
                        owner * CAP : owner * CAP + CAP, u * UNIT : u * UNIT + UNIT
                    ]
            return carry

        lax.fori_loop(0, 4 * STAGES, one, 0)
        return links.copy(
            work.at[rows_at(((1 - core) * 4 + chip) * (STAGES * block), STAGES * block)],
            partner.at[rows_at(chip * (STAGES * block), STAGES * block)],
            other_core(),
        )

    def join(chip, made):
        made.wait_recv()
        add_into(
            work.at[rows_at((core * 4 + chip) * (STAGES * block), STAGES * block)],
            partner.at[rows_at(chip * (STAGES * block), STAGES * block)],
        )

    rings_y = [
        RingSum(
            links,
            "y",
            work,
            core * (4 * STAGES * block) + s * block,
            block,
            STAGES * block,
            first_y.at[pl.ds(s * block, block)],
            second_y.at[pl.ds(s * 2 * block, 2 * block)],
        )
        for s in range(STAGES)
    ]
    held(2, ("pair", "near"))
    for made in scale_pair:
        made.wait_recv()
    gate_and_up(2, above)
    sum_above = down(above)
    gate_and_up(2, below)
    gather_far(2)
    sum_below = down(below)
    join(above, sum_above)
    for ring in rings_y:
        ring.direct_up()
    held(2, ("far",))
    gate_and_up(2, far)
    sum_far = down(far)
    join(below, sum_below)
    for ring in rings_y:
        ring.direct_down()
    gate_and_up(2, y)
    join(far, sum_far)
    for ring in rings_y:
        ring.opposite()
    sum_own = down(y)
    join(y, sum_own)

    back_moves = []

    def give_back(s):
        rings_y[s].arrived()

        def one(g, carry):
            total = rings_y[s].total(g * CAP, CAP).astype(BF16).astype(F32)
            pieces[rows_at((s * EXPERTS + g) * CAP, CAP), :] = (total * share).astype(BF16)
            return carry

        lax.fori_loop(0, EXPERTS, one, 0)
        lands = back.at[rows_at(me * CAP, CAP), pl.ds(s * UNIT, UNIT)]
        for step in range(1, EXPERTS):
            to = (me + step) % EXPERTS
            piece = pieces.at[rows_at((s * EXPERTS + to) * CAP, CAP)]
            back_moves.append(links.copy(piece, lands, exp_peer(step)))
        lands[...] = pieces[rows_at((s * EXPERTS + me) * CAP, CAP), :]

    rings_y[0].relay()
    rings_y[1].relay()
    rings_y[2].relay()
    give_back(0)
    give_back(1)
    give_back(2)
    for made in back_moves:
        made.wait_recv()
    summed = lax.dot_general(table[...], back[...], first, preferred_element_type=F32)
    hidden[...] = (hidden[...].astype(F32) + summed).astype(BF16)

    out_moves = []
    for step in range(1, EXPERTS):
        to = (me + step) % EXPERTS
        out_moves.append(
            links.copy(hidden.at[rows_at(to * 32, 32)], rows_out.at[me], exp_peer(step))
        )
    rows_out[me] = hidden[rows_at(me * 32, 32), :]
    for made in out_moves:
        made.wait_recv()

    def put(g, carry):
        for s in range(STAGES):
            out_ref[:, unit_cols(s * EXPERTS + g)] = rows_out[g, :, pl.ds(s * UNIT, UNIT)]
        return carry

    lax.fori_loop(0, EXPERTS, put, 0)
    links.drain()

    @pl.when(core == 0)
    def _():
        state_pair().wait_send()

    for step in range(1, 4):

        @pl.when((core == 1) & (y + step < 4))
        def _(step=step):
            state_up(step).wait_send()

        @pl.when((core == 1) & (y >= step))
        def _(step=step):
            state_over(step).wait_send()


def layer(*arrays):
    vmem = pl.BlockSpec(memory_space=pltpu.VMEM)
    hbm = pl.BlockSpec(memory_space=pl.ANY)

    def rows(n, width=UNIT):
        return pltpu.VMEM((n, width), BF16)

    block = EXPERTS * CAP
    return pl.pallas_call(
        layer_kernel,
        out_shape=jax.ShapeDtypeStruct((32, 6144), BF16),
        in_specs=[vmem] * 5 + [hbm, vmem, vmem, vmem, vmem, hbm, hbm, hbm],
        out_specs=vmem,
        scratch_shapes=[
            rows(528),
            rows(528),
            pltpu.VMEM((4, 528, 128), BF16),
            pltpu.VMEM((512, 128), F32),
            pltpu.VMEM((4, 128), F32),
            rows(512, 512),
            pltpu.VMEM((4, 576, 1536), BF16),
            rows(1152, 6144),
            rows(24 * block),
            rows(6 * 2048),
            rows(6 * 1024),
            rows(6 * 256),
            rows(6 * 512),
            pltpu.VMEM((EXPERTS, 32, STAGES * UNIT), BF16),
            rows(512, STAGES * UNIT),
            rows(512, STAGES * UNIT),
            rows(block, 512),
            rows(STAGES * block),
            rows(CAP, 6144),
            rows(8 * CAP, 6144),
            pltpu.VMEM((8 * CAP, UNIT), F32),
            pltpu.VMEM((8 * CAP, 1152), F32),
            rows(2 * CAP, 576),
            rows(4 * STAGES * block),
            rows(STAGES * block),
            rows(2 * STAGES * block),
            rows(block, STAGES * UNIT),
            pltpu.VMEM((EXPERTS, 32, STAGES * UNIT), BF16),
            pltpu.SemaphoreType.DMA((7,)),
            pltpu.SemaphoreType.DMA((LINKS,)),
            pltpu.SemaphoreType.DMA((LINKS,)),
            pltpu.SemaphoreType.DMA((8,)),
            pltpu.SemaphoreType.DMA((8,)),
        ],
        compiler_params=pltpu.CompilerParams(
            collective_id=0, has_side_effects=True, vmem_limit_bytes=65000 << 10
        ),
        name="layer",
    )(*arrays)


def per_device(
    query_rows,
    key_rows,
    value_rows,
    log_decay,
    attn_gain,
    out_weight,
    residual,
    ffn_gain,
    router,
    expert_ids,
    w_gate,
    w_up,
    w_down,
):
    return layer(
        query_rows,
        key_rows,
        value_rows,
        log_decay.T,
        attn_gain.reshape(1, -1),
        out_weight,
        residual,
        expert_ids.T,
        ffn_gain.reshape(1, -1),
        router.T,
        w_gate[0].T,
        w_up[0].T,
        w_down[0],
    )


def solution(mesh):
    return jax.shard_map(
        per_device,
        mesh=mesh,
        in_specs=(
            P("ctx", "exp"),
            P("ctx", "exp"),
            P("ctx", "exp"),
            P("ctx", "exp"),
            P("exp"),
            P("exp", "ctx"),
            P(("ctx", "exp"), None),
            P(),
            P(),
            P("ctx", None),
            P("exp", None, "ctx"),
            P("exp", None, "ctx"),
            P("exp", "ctx", None),
        ),
        out_specs=P(("ctx", "exp"), None),
        check_vma=False,
    )
```

time: 464 us -> 183 us (0.39)
  waiting for transfers between devices: 365 us -> 0 us
  Pallas kernels: 0 us -> 181 us
  matrix products: 62.3 us -> 0 us
  between operations: 13.6 us -> 0.01 us
  blocking collectives: 10.8 us -> 0 us
  other arithmetic: 7.34 us -> 0 us
    reduce_scatter x3 -> x0, waiting for transfers between devices: 205 us -> none  [the longest x1 81.8 us: per_device(): lax.psum_scatter(jnp.dot(attn_out, out_full, preferred_element_type=jnp.f...]
    pallas_call x0 -> x1, Pallas kernels: none -> 181 us  [layer(): pl.pallas_call(layer_kernel, out_shape=jax.ShapeDtypeStruct((32, 6144), B...]
    all_gather x4 -> x0, waiting for transfers between devices: 159 us -> none  [the longest x1 60.1 us: per_device(): lax.all_gather(row_norm(hidden_rows, ffn_gain), 'exp', axis=0, tiled=True)]
    dot_general x10 -> x0, matrix products: 62.3 us -> none  [the longest x1 10.9 us: per_device(): gate = jnp.dot(piece, gate_cols, preferred_element_type=jnp.float32)]
    all_gather x1 -> x0, blocking collectives: 10.8 us -> none  [prefix(): lax.all_gather(a.astype(kind), axis)]
  transfers between devices with their start and end apart: 7 -> 0, of which waited for: 7 -> 0; matrix products, arithmetic and copies ran while one was open for 3% -> 0% of each run, Pallas kernels for 0% -> 0%
where the time goes in v2:
time: 183 us
  Pallas kernels  181 us (99%)
    pallas_call x1, Pallas kernels, layer(): pl.pallas_call(layer_kernel, out_shape=jax.ShapeDtypeStruct((32, 6144), B...  181 us

profile of v2, /device:TPU:0, one launch (start us, length us, event | category | flops | bytes accessed | tf_op | source)
XLA Modules:
  0.0 183.0 jit_solution(10801905713923923527)
XLA Ops:
  0.0 181.2 %layer.1 = bf16[32,6144]{1,0:T(8,128)(2,1)} custom-call(bf16[512,512]{1,0:T(8,128)(2,1)} %query_ref.1, bf16[512,512]{1,0:T(8,128)(2,1)} %key_ref.1, bf16[512,512]{1,0:T(8,128)(2,1)} %value_ref.1, f32[4,512]{1,0:T(4,128)} %bitcast.17, f32[1,512]{1,0:T(1,128)} %bitcast.19, bf16[512,768]{1,0:T(8,128)(2,1)} %out_w_ref.1, bf16[32,6144]{1,0:T(8,128)(2,1)} %resid_ref.1, ...), custom_call_target="tpu_custom_call" | custom-call | tf_op jit(solution)/shard_map/layer/pallas_call | solution.py:852
  181.2 1.8 copy.15

commit v3 on v2

--- a/solution.py
+++ b/solution.py
@@ -14,7 +14,7 @@
 CAP = 80
 UNIT = 128
 STAGES = 3
-LINKS = 288
+LINKS = 304
 
 
 def place():
@@ -49,7 +49,7 @@
 class Links:
     def __init__(self, send, recv):
         self.send, self.recv, self.count = send, recv, 0
-        self.open, self.done = [], 0
+        self.open, self.group, self.early = {}, "w", None
 
     def copy(self, src, dst, device):
         made = pltpu.make_async_remote_copy(
@@ -63,14 +63,13 @@
         made.start()
         self.count += 1
         assert self.count <= LINKS
-        self.open.append(made)
+        self.open.setdefault(self.group, []).append(made)
         return made
 
-    def drain(self, until=None):
-        until = self.count if until is None else until
-        for made in self.open[self.done : until]:
-            made.wait_send()
-        self.done = max(self.done, until)
+    def drain(self, group):
+        for made in self.open.pop(group, []):
+            if made is not self.early:
+                made.wait_send()
 
 
 def add_into(target, extra):
@@ -137,6 +136,31 @@
         own = self.part[rows_at(self.base + self.i * self.stride + start, size), :].astype(F32)
         own = own + self.second[rows_at(start, size), :].astype(F32)
         return own + self.second[rows_at(self.n + start, size), :].astype(F32)
+
+
+class DirectSum:
+    def __init__(self, links, axis, part, base, n, landed):
+        place_of = dict(zip(("y", "core", "x", "z"), place()))
+        self.links, self.axis, self.i = links, axis, place_of[axis]
+        self.part, self.base, self.n, self.landed = part, base, n, landed
+
+    def send(self):
+        self.moves = [
+            self.links.copy(
+                self.part.at[rows_at(self.base + (self.i + step) % 4 * self.n, self.n)],
+                self.landed.at[pl.ds((step - 1) * self.n, self.n)],
+                along(self.axis, step),
+            )
+            for step in (2, 1, 3)
+        ]
+
+    def total(self):
+        for made in self.moves:
+            made.wait_recv()
+        total = self.part[rows_at(self.base + self.i * self.n, self.n), :].astype(F32)
+        for k in range(3):
+            total = total + self.landed[pl.ds(k * self.n, self.n), :].astype(F32)
+        return total
 
 
 def columns(start, size):
@@ -169,6 +193,11 @@
     up_ref,
     down_ref,
     out_ref,
+    query,
+    key,
+    value,
+    resid,
+    routes,
     state,
     chip_state,
     states,
@@ -180,8 +209,7 @@
     work,
     second,
     half,
-    last_first,
-    last_second,
+    last,
     resid_parts,
     resid_cols,
     hidden,
@@ -217,21 +245,36 @@
         chip = (y + k + k // 2 - 2 * (k // 3)) % 4
         return columns(chip * 1536 + j % 12 * UNIT, UNIT)
 
-    load_gate = pltpu.make_async_copy(gate_ref, gate_up.at[pl.ds(0, 576)], local.at[1])
-    load_up = pltpu.make_async_copy(up_ref, gate_up.at[pl.ds(576, 576)], local.at[2])
-    w_all, w_low, w_high = pl.ds(0, 512), pl.ds(0, 256), pl.ds(256, 256)
-
-    def w_part(chip, side, rows):
-        return wide.at[chip, rows, columns(side * 768, 768)]
-
-    load_w = pltpu.make_async_copy(out_w_ref, w_part(y, core, w_all), local.at[0])
-    load_w.start()
-
     barrier = pltpu.get_barrier_semaphore()
     for device in [along("y", 1), along("y", 3), other_core(), along("y", 2)]:
         pl.semaphore_signal(barrier, inc=1, device_id=device, device_id_type=MESH)
     for step in range(1, EXPERTS):
         pl.semaphore_signal(barrier, inc=1, device_id=exp_peer(step), device_id_type=MESH)
+
+    load_gate = pltpu.make_async_copy(gate_ref, gate_up.at[pl.ds(0, 576)], local.at[1])
+    load_up = pltpu.make_async_copy(up_ref, gate_up.at[pl.ds(576, 576)], local.at[2])
+    w_all, w_low, w_high = pl.ds(0, 512), pl.ds(0, 256), pl.ds(256, 256)
+    one_way, other_way = (2 * core + 3) % 4, (2 * core + 1) % 4
+    one_chip, other_chip = (y + one_way) % 4, (y + other_way) % 4
+
+    def w_part(chip, side, rows):
+        return wide.at[chip, rows, columns(side * 768, 768)]
+
+    load_in = []
+    for k, (src, dst) in enumerate(
+        (
+            (key_ref, key),
+            (value_ref, value),
+            (query_ref, query),
+            (resid_ref, resid),
+            (router_ref, routes),
+        )
+    ):
+        made = pltpu.make_async_copy(src, dst, local.at[7 + k])
+        made.start()
+        load_in.append(made)
+    load_w = pltpu.make_async_copy(out_w_ref, w_part(y, core, w_all), local.at[0])
+    load_w.start()
 
     earlier = lax.broadcasted_iota(jnp.int32, (512, 512), 1) <= lax.broadcasted_iota(
         jnp.int32, (512, 512), 0
@@ -244,14 +287,16 @@
     for term in split3(decay_ref[...]):
         run_col = run_col + lax.dot_general(lower, term, turned, preferred_element_type=F32)
         run_row = run_row + lax.dot_general(term, lower, turned, preferred_element_type=F32)
+    load_in[0].wait()
+    load_in[1].wait()
     lines = lax.broadcasted_iota(jnp.int32, (4, 128), 0)
     ends = jnp.zeros((4, 128), F32)
     for h in range(4):
         lanes = pl.ds(h * 128, 128)
         end = run_col[511:512, h : h + 1]
         to_end = jnp.exp(end - run_col[:, h : h + 1])
-        decayed = (key_ref[:, lanes].astype(F32) * to_end).astype(BF16)
-        own = lax.dot_general(decayed, value_ref[:, lanes], first, preferred_element_type=F32)
+        decayed = (key[:, lanes].astype(F32) * to_end).astype(BF16)
+        own = lax.dot_general(decayed, value[:, lanes], first, preferred_element_type=F32)
         state[pl.ds(h * 128, 128), :] = own.astype(BF16)
         ends = jnp.where(lines == h, end, ends)
 
@@ -286,44 +331,45 @@
     def state_over(step):
         return state_copy(states.at[step], states.at[step], 4 + step, other_core())
 
+    state_pair().start()
+
+    def spread_w(chip, rows, device):
+        src = out_w_ref if chip is None else w_part(chip, core, rows)
+        return links.copy(src, w_part(y if chip is None else chip, core, rows), device)
+
+    w_first = spread_w(None, w_all, along("y", one_way))
+    w_pair = [spread_w(None, w_all, other_core())]
+
+    state_pair().wait_recv()
+
     @pl.when(core == 0)
     def _():
-        state_pair().start()
-
-    def spread_w(chip, side, rows, device, own=False):
-        return links.copy(out_w_ref.at[rows] if own else w_part(chip, side, rows), w_part(chip, side, rows), device)
-
-    w_up_low = spread_w(y, core, w_low, along("y", 1), True)
-    w_down_high = spread_w(y, core, w_high, along("y", -1), True)
-    w_pair = [spread_w(y, core, w_all, other_core(), True)]
-
-    @pl.when(core == 1)
-    def _():
-        state_pair().wait_recv()
-        own_ends = ends_of(state)
+        pair_ends = ends_of(states.at[0])
         for h in range(4):
             rows = pl.ds(h * 128, 128)
-            joined = jnp.exp(own_ends[h : h + 1]) * states[0, rows, :].astype(F32)
-            chip_state[rows, :] = (joined + state[rows, :].astype(F32)).astype(BF16)
-        chip_state[pl.ds(512, 16), :] = pack_ends(own_ends + ends_of(states.at[0]))
+            joined = jnp.exp(pair_ends[h : h + 1]) * state[rows, :].astype(F32)
+            chip_state[rows, :] = (joined + states[0, rows, :].astype(F32)).astype(BF16)
+        chip_state[pl.ds(512, 16), :] = pack_ends(pair_ends + ends_of(state))
         for step in range(1, 4):
 
             @pl.when(y + step < 4)
             def _(step=step):
                 state_up(step).start()
 
-    w_up_high = spread_w(y, core, w_high, along("y", 1), True)
-    w_down_low = spread_w(y, core, w_low, along("y", -1), True)
     load_gate.start()
     load_up.start()
 
+    for made in load_in[2:]:
+        made.wait()
+
     def resid_part(g, carry):
         for s in range(STAGES):
-            resid_parts[g, :, pl.ds(s * UNIT, UNIT)] = resid_ref[:, unit_cols(s * EXPERTS + g)]
+            resid_parts[g, :, pl.ds(s * UNIT, UNIT)] = resid[:, unit_cols(s * EXPERTS + g)]
         return carry
 
     lax.fori_loop(0, EXPERTS, resid_part, 0)
     resid_moves = []
+    links.group = "rows"
     for step in range(1, EXPERTS):
         to = (me + step) % EXPERTS
         resid_moves.append(
@@ -337,8 +383,8 @@
             seen = (r + 1) * 256
             rows = pl.ds(r * 256, 256)
             scores = lax.dot_general(
-                query_ref[rows, lanes],
-                key_ref[pl.ds(0, seen), lanes],
+                query[rows, lanes],
+                key[pl.ds(0, seen), lanes],
                 turned,
                 preferred_element_type=F32,
             )
@@ -348,23 +394,24 @@
             decay = jnp.where(late >= soon, jnp.exp(jnp.minimum(spread_of, 0.0)), 0.0)
             sums[rows, lanes] = jnp.dot(
                 (scores * decay).astype(BF16),
-                value_ref[pl.ds(0, seen), lanes],
+                value[pl.ds(0, seen), lanes],
                 preferred_element_type=F32,
             )
 
     for step in range(1, 4):
 
-        @pl.when((core == 1) & (y >= step))
+        @pl.when((core == 0) & (y >= step))
         def _(step=step):
             state_up(step).wait_recv()
             state_over(step).start()
 
-    w_up_low.wait_recv()
-    w_on_up = spread_w(below, core, w_low, along("y", 1))
-    w_pair.append(spread_w(below, core, w_low, other_core()))
-    w_down_high.wait_recv()
-    w_on_down = spread_w(above, core, w_high, along("y", -1))
-    w_pair.append(spread_w(above, core, w_high, other_core()))
+    links.group = "w"
+    w_first.wait_send()
+    links.early = w_first
+    w_second = spread_w(None, w_all, along("y", other_way))
+    w_first.wait_recv()
+    w_near = spread_w(other_chip, w_all, other_core())
+    w_far = [spread_w(other_chip, w_low, along("y", one_way))]
 
     experts = lax.broadcasted_iota(jnp.int32, (EXPERTS, 512), 0)
     picked = (ids_ref[0:1, :] == experts) | (ids_ref[1:2, :] == experts)
@@ -387,7 +434,7 @@
     gone[...] = jnp.zeros((4, 128), F32)
     for step in range(1, 4):
 
-        @pl.when((core == 0) & (y >= step))
+        @pl.when((core == 1) & (y >= step))
         def _(step=step):
             state_over(step).wait_recv()
 
@@ -412,7 +459,7 @@
         full = carried[lanes, :]
         near = full.astype(BF16)
         rest = (full - near.astype(F32)).astype(BF16)
-        asked = query_ref[:, lanes]
+        asked = query[:, lanes]
         cross = jnp.dot(asked, near, preferred_element_type=F32)
         cross = cross + jnp.dot(asked, rest, preferred_element_type=F32)
         total = sums[pl.ds(0, 512), lanes] + jnp.exp(run_col[:, h : h + 1]) * cross
@@ -421,11 +468,8 @@
             total * lax.rsqrt(mean + 1e-06) * head_gain_ref[:, lanes]
         ).astype(BF16)
 
-    w_up_high.wait_recv()
-    w_pair.append(spread_w(below, core, w_high, other_core()))
-    w_down_low.wait_recv()
-    w_pair.append(spread_w(above, core, w_low, other_core()))
     load_w.wait()
+    w_near.wait_recv()
     for made in w_pair:
         made.wait_recv()
 
@@ -445,19 +489,10 @@
                     second.at[pl.ds(k * 2048, 2048)],
                 )
             )
-        for which, (rings, axis) in enumerate(((lasts_a, "z"), (lasts_b, "x"))):
+        for which, (sums_of, axis) in enumerate(((lasts_a, "z"), (lasts_b, "x"))):
             k = which * STAGES + s
-            rings.append(
-                RingSum(
-                    links,
-                    axis,
-                    half,
-                    k * 1024,
-                    256,
-                    256,
-                    last_first.at[pl.ds(k * 256, 256)],
-                    last_second.at[pl.ds(k * 512, 512)],
-                )
+            sums_of.append(
+                DirectSum(links, axis, half, k * 1024, 256, last.at[pl.ds(k * 768, 768)])
             )
 
     def project_quad(s, to):
@@ -482,6 +517,7 @@
             project_quad(s, (x + 3 + i) % 4)
             return carry
 
+        links.group = "sum"
         project_quad(s, (x + 2) % 4)
         rings_a[s].opposite()
         lax.fori_loop(0, 3, one, 0)
@@ -492,44 +528,39 @@
         rings_b[s].direct_down()
 
     def relay(s):
+        links.group = "sum"
         rings_a[s].relay()
         rings_b[s].relay()
 
     def turn(s):
-        for ring, last in ((rings_a[s], lasts_a[s]), (rings_b[s], lasts_b[s])):
+        links.group = "sum"
+        for ring, last_of in ((rings_a[s], lasts_a[s]), (rings_b[s], lasts_b[s])):
             ring.arrived()
 
-            def one(u, carry, ring=ring, last=last):
+            def one(u, carry, ring=ring, last_of=last_of):
                 for side in range(2):
-                    rows = rows_at(last.base + u * 256 + side * 128, 128)
+                    rows = rows_at(last_of.base + u * 256 + side * 128, 128)
                     half[rows, :] = ring.total(side * 512 + u * 128, 128).astype(BF16)
                 return carry
 
             lax.fori_loop(0, 4, one, 0)
-            last.opposite()
-            last.direct_up()
-            last.direct_down()
-
-    def turn_relay(s):
-        lasts_a[s].relay()
-        lasts_b[s].relay()
+            last_of.send()
 
     row_moves = [[] for _ in range(STAGES)]
+    block = EXPERTS * CAP
 
     def dispatch(s):
         cols = pl.ds(s * UNIT, UNIT)
         if s == 0:
             for made in resid_moves:
                 made.wait_recv()
-        for start, ring in ((0, lasts_a[s]), (256, lasts_b[s])):
-            ring.arrived()
-            rows = pl.ds(start, 256)
-            hidden[rows, cols] = (
-                ring.total(0, 256) + resid_cols[rows, cols].astype(F32)
-            ).astype(BF16)
-        found = jnp.dot(table[...], hidden[:, cols], preferred_element_type=F32)
-        pieces[pl.ds(s * EXPERTS * CAP, EXPERTS * CAP), :] = found.astype(BF16)
-        lands = rows_in.at[:, columns((s * EXPERTS + me) * UNIT, UNIT)]
+        links.group = "rows"
+        for start, last_of in ((0, lasts_a[s]), (256, lasts_b[s])):
+            total = last_of.total() + resid_cols[pl.ds(start, 256), cols].astype(F32)
+            hidden[pl.ds(s * 512 + start, 256), :] = total.astype(BF16)
+        found = jnp.dot(table[...], hidden[pl.ds(s * 512, 512), :], preferred_element_type=F32)
+        pieces[pl.ds(s * block, block), :] = found.astype(BF16)
+        lands = rows_in.at[rows_at((s * EXPERTS + me) * CAP, CAP)]
         for step in range(1, EXPERTS):
             to = (me + step) % EXPERTS
             piece = pieces.at[rows_at((s * EXPERTS + to) * CAP, CAP)]
@@ -550,9 +581,10 @@
     def gather(s):
         for made in row_moves[s]:
             made.wait_recv()
+        links.group = "gather"
         for u in range(EXPERTS):
             cols = pl.ds((s * EXPERTS + u) * UNIT, UNIT)
-            part = rows_in[:, cols].astype(F32)
+            part = rows_in[pl.ds((s * EXPERTS + u) * CAP, CAP), :].astype(F32)
             squares[0] = squares[0] + jnp.sum(part * part, axis=1, keepdims=True)
             tokens[mine, cols] = (part * gain_ref[:, unit_cols(s * EXPERTS + u)]).astype(BF16)
         gathers[s] = dict(
@@ -566,6 +598,7 @@
     from_below, from_above, from_far = below * 2 + core, above * 2 + core, far * 2 + core
 
     def gather_mid(s):
+        links.group = "gather"
         g = gathers[s]
         g["up_low"].wait_recv()
         g["on_up"] = spread(s, from_below, 0, along("y", 1))
@@ -575,6 +608,7 @@
         g["near"].append(spread(s, from_above, 1, other_core()))
 
     def gather_near(s):
+        links.group = "gather"
         g = gathers[s]
         g["up_high"].wait_recv()
         g["near"].append(spread(s, from_below, 1, other_core()))
@@ -582,6 +616,7 @@
         g["near"].append(spread(s, from_above, 0, other_core()))
 
     def gather_far(s):
+        links.group = "gather"
         g = gathers[s]
         g["on_up"].wait_recv()
         g["far"] = [spread(s, from_far, 0, other_core())]
@@ -617,42 +652,37 @@
         gate, upper = total[:, :576], total[:, 576:]
         active[...] = (gate / (1.0 + jnp.exp(-gate)) * upper).astype(BF16)
 
-    def gate_and_up_all(s):
-        def one(chip, carry):
-            gate_and_up(s, chip)
-            return carry
-
-        lax.fori_loop(0, 4, one, 0)
-
     project(0)
     relay(0)
+    links.group = "w"
+    w_second.wait_recv()
+    w_next = spread_w(one_chip, w_all, other_core())
+    w_far.append(spread_w(one_chip, w_high, along("y", other_way)))
+    w_next.wait_recv()
     project(1)
     turn(0)
-    w_on_up.wait_recv()
-    w_pair_far = [spread_w(far, core, w_low, other_core())]
-    w_on_down.wait_recv()
-    w_pair_far.append(spread_w(far, core, w_high, other_core()))
+    links.group = "w"
+    w_far_near = []
+    for made, rows in zip(w_far, (w_low, w_high)):
+        made.wait_recv()
+        w_far_near.append(spread_w(far, rows, other_core()))
     relay(1)
-    turn_relay(0)
-    for made in w_pair_far:
+    dispatch(0)
+    turn(1)
+    for made in w_far_near:
         made.wait_recv()
     project(2)
-    dispatch(0)
-    turn(1)
-    relay(2)
-    turn_relay(1)
     gather(0)
     dispatch(1)
+    relay(2)
+    gather_mid(0)
+    gather(1)
     turn(2)
-    gather_mid(0)
-    turn_relay(2)
-    gather(1)
     gather_near(0)
-    dispatch(2)
-    sent_rows = links.count
     gather_far(0)
     gather_mid(1)
-    links.drain(sent_rows)
+    dispatch(2)
+    links.drain("w")
     load_down = []
     for k in range(4):
         made = pltpu.make_async_copy(
@@ -663,6 +693,11 @@
     load_gate.wait()
     load_up.wait()
     held(0, ("pair", "near", "far"))
+    gate_and_up(0, y)
+    gate_and_up(0, above)
+    gather_near(1)
+    gate_and_up(0, below)
+    gather_far(1)
     gather(2)
 
     def spread_scale(block, device):
@@ -673,21 +708,96 @@
     scales[mine, :] = jnp.broadcast_to(scale, (CAP, UNIT))
     scale_up = spread_scale(ctx, along("y", 1))
     scale_down = spread_scale(ctx, along("y", -1))
-    scale_pair = [spread_scale(ctx, other_core())]
-    gather_near(1)
-    gather_far(1)
-    gate_and_up_all(0)
+    scale_own = spread_scale(ctx, other_core())
+    def owned(owner, chip, s):
+        return work.at[rows_at(((owner * 4 + chip) * STAGES + s) * block, block)]
+
+    def down(chip):
+        moves = []
+        for s in range(STAGES):
+
+            def one(quad, carry):
+                k = quad // 3
+                part = (chip + k + k // 2 - 2 * (k // 3)) % 4
+                w = wide[part, :, columns(quad % 3 * 512, 512)]
+                o = jnp.dot(active[...], w, preferred_element_type=F32).astype(BF16)
+                for owner in range(2):
+                    for u in range(4):
+                        start = (owner * 4 + chip) * (STAGES * block) + (quad * 4 + u) * CAP
+                        work[rows_at(start, CAP), :] = o[
+                            owner * CAP : owner * CAP + CAP, u * UNIT : u * UNIT + UNIT
+                        ]
+                return carry
+
+            lax.fori_loop(4 * s, 4 * s + 4, one, 0)
+            lands = partner.at[rows_at((chip * STAGES + s) * block, block)]
+            moves.append(links.copy(owned(1 - core, chip, s), lands, other_core()))
+        return moves
+
+    def join(chip, moves, s):
+        moves[s].wait_recv()
+        add_into(owned(core, chip, s), partner.at[rows_at((chip * STAGES + s) * block, block)])
+
+    rings_y = [
+        RingSum(
+            links,
+            "y",
+            work,
+            core * (4 * STAGES * block) + s * block,
+            block,
+            STAGES * block,
+            first_y.at[pl.ds(s * block, block)],
+            second_y.at[pl.ds(s * 2 * block, 2 * block)],
+        )
+        for s in range(STAGES)
+    ]
+    held(1, ("pair", "near", "far"))
+    gate_and_up(1, y)
+    held(2, ("pair",))
+    scale_own.wait_recv()
+    gate_and_up(2, y)
     gather_mid(2)
     scale_up.wait_recv()
     scale_on = spread_scale(from_below, along("y", 1))
-    scale_pair.append(spread_scale(from_below, other_core()))
+    scale_pair = [spread_scale(from_below, other_core())]
     scale_down.wait_recv()
     scale_pair.append(spread_scale(from_above, other_core()))
-    held(1, ("pair", "near", "far"))
-    gate_and_up_all(1)
+    links.drain("sum")
+    for made in load_down:
+        made.wait()
+    links.group = "rest"
+    sum_own = down(y)
     gather_near(2)
     scale_on.wait_recv()
-    scale_pair.append(spread_scale(from_far, other_core()))
+    scale_far = spread_scale(from_far, other_core())
+    gate_and_up(0, far)
+    gate_and_up(1, far)
+    gather_far(2)
+    links.group = "rest"
+    gate_and_up(1, above)
+    held(2, ("far",))
+    scale_far.wait_recv()
+    gate_and_up(2, far)
+    sum_far = down(far)
+    for s in range(STAGES):
+        join(far, sum_far, s)
+        rings_y[s].opposite()
+    held(2, ("near",))
+    for made in scale_pair:
+        made.wait_recv()
+    gate_and_up(2, above)
+    sum_above = down(above)
+    gate_and_up(1, below)
+    gate_and_up(2, below)
+    for s in range(STAGES):
+        join(above, sum_above, s)
+        rings_y[s].direct_up()
+    sum_below = down(below)
+    for s in range(STAGES):
+        join(below, sum_below, s)
+        rings_y[s].direct_down()
+    for s in range(STAGES):
+        join(y, sum_own, s)
 
     my_ids = lax.dot_general(
         table[rows_at(me * CAP, CAP), :],
@@ -697,7 +807,7 @@
     )
     logits = jnp.zeros((CAP, EXPERTS), F32)
     for k in range(4):
-        part = router_ref[:, columns(chip_at(y, k) * 1536, 1536)]
+        part = routes[:, columns(chip_at(y, k) * 1536, 1536)]
         router_high = part.astype(BF16)
         router_low = (part - router_high.astype(F32)).astype(BF16)
         token = tokens[mine, pl.ds(k * 1536, 1536)]
@@ -709,77 +819,12 @@
     both = (my_ids[:, 0:1] == lanes_f) | (my_ids[:, 1:2] == lanes_f)
     total = jnp.sum(jnp.where(both, gates, 0.0), axis=1, keepdims=True)
     share = jnp.sum(jnp.where(lanes == me, gates, 0.0), axis=1, keepdims=True) / total
-
-    block = EXPERTS * CAP
-    for made in load_down:
-        made.wait()
-
-    def down(chip):
-        def one(quad, carry):
-            k = quad // 3
-            part = (chip + k + k // 2 - 2 * (k // 3)) % 4
-            w = wide[part, :, columns(quad % 3 * 512, 512)]
-            o = jnp.dot(active[...], w, preferred_element_type=F32).astype(BF16)
-            for owner in range(2):
-                for u in range(4):
-                    start = (owner * 4 + chip) * (STAGES * block) + (quad * 4 + u) * CAP
-                    work[rows_at(start, CAP), :] = o[
-                        owner * CAP : owner * CAP + CAP, u * UNIT : u * UNIT + UNIT
-                    ]
-            return carry
-
-        lax.fori_loop(0, 4 * STAGES, one, 0)
-        return links.copy(
-            work.at[rows_at(((1 - core) * 4 + chip) * (STAGES * block), STAGES * block)],
-            partner.at[rows_at(chip * (STAGES * block), STAGES * block)],
-            other_core(),
-        )
-
-    def join(chip, made):
-        made.wait_recv()
-        add_into(
-            work.at[rows_at((core * 4 + chip) * (STAGES * block), STAGES * block)],
-            partner.at[rows_at(chip * (STAGES * block), STAGES * block)],
-        )
-
-    rings_y = [
-        RingSum(
-            links,
-            "y",
-            work,
-            core * (4 * STAGES * block) + s * block,
-            block,
-            STAGES * block,
-            first_y.at[pl.ds(s * block, block)],
-            second_y.at[pl.ds(s * 2 * block, 2 * block)],
-        )
-        for s in range(STAGES)
-    ]
-    held(2, ("pair", "near"))
-    for made in scale_pair:
-        made.wait_recv()
-    gate_and_up(2, above)
-    sum_above = down(above)
-    gate_and_up(2, below)
-    gather_far(2)
-    sum_below = down(below)
-    join(above, sum_above)
-    for ring in rings_y:
-        ring.direct_up()
-    held(2, ("far",))
-    gate_and_up(2, far)
-    sum_far = down(far)
-    join(below, sum_below)
-    for ring in rings_y:
-        ring.direct_down()
-    gate_and_up(2, y)
-    join(far, sum_far)
-    for ring in rings_y:
-        ring.opposite()
-    sum_own = down(y)
-    join(y, sum_own)
-
-    back_moves = []
+    share = jnp.broadcast_to(share, (CAP, UNIT))
+
+    links.drain("rows")
+
+    back_moves = [[] for _ in range(STAGES)]
+    out_moves = []
 
     def give_back(s):
         rings_y[s].arrived()
@@ -790,53 +835,57 @@
             return carry
 
         lax.fori_loop(0, EXPERTS, one, 0)
-        lands = back.at[rows_at(me * CAP, CAP), pl.ds(s * UNIT, UNIT)]
+        lands = back.at[rows_at((s * EXPERTS + me) * CAP, CAP)]
         for step in range(1, EXPERTS):
             to = (me + step) % EXPERTS
             piece = pieces.at[rows_at((s * EXPERTS + to) * CAP, CAP)]
-            back_moves.append(links.copy(piece, lands, exp_peer(step)))
+            back_moves[s].append(links.copy(piece, lands, exp_peer(step)))
         lands[...] = pieces[rows_at((s * EXPERTS + me) * CAP, CAP), :]
+
+    def combine(s):
+        for made in back_moves[s]:
+            made.wait_recv()
+        summed = lax.dot_general(
+            table[...], back[pl.ds(s * block, block), :], first, preferred_element_type=F32
+        )
+        rows = pl.ds(s * 512, 512)
+        hidden[rows, :] = (hidden[rows, :].astype(F32) + summed).astype(BF16)
+        for step in range(1, EXPERTS):
+            to = (me + step) % EXPERTS
+            part = hidden.at[rows_at(s * 512 + to * 32, 32)]
+            out_moves.append(links.copy(part, rows_out.at[s, me], exp_peer(step)))
+        rows_out[s, me] = hidden[rows_at(s * 512 + me * 32, 32), :]
 
     rings_y[0].relay()
     rings_y[1].relay()
     rings_y[2].relay()
     give_back(0)
     give_back(1)
+    combine(0)
     give_back(2)
-    for made in back_moves:
-        made.wait_recv()
-    summed = lax.dot_general(table[...], back[...], first, preferred_element_type=F32)
-    hidden[...] = (hidden[...].astype(F32) + summed).astype(BF16)
-
-    out_moves = []
-    for step in range(1, EXPERTS):
-        to = (me + step) % EXPERTS
-        out_moves.append(
-            links.copy(hidden.at[rows_at(to * 32, 32)], rows_out.at[me], exp_peer(step))
-        )
-    rows_out[me] = hidden[rows_at(me * 32, 32), :]
+    combine(1)
+    combine(2)
     for made in out_moves:
         made.wait_recv()
 
     def put(g, carry):
         for s in range(STAGES):
-            out_ref[:, unit_cols(s * EXPERTS + g)] = rows_out[g, :, pl.ds(s * UNIT, UNIT)]
+            out_ref[:, unit_cols(s * EXPERTS + g)] = rows_out[s, g]
         return carry
 
     lax.fori_loop(0, EXPERTS, put, 0)
-    links.drain()
-
-    @pl.when(core == 0)
-    def _():
-        state_pair().wait_send()
+    links.drain("gather")
+    links.drain("rest")
+
+    state_pair().wait_send()
 
     for step in range(1, 4):
 
-        @pl.when((core == 1) & (y + step < 4))
+        @pl.when((core == 0) & (y + step < 4))
         def _(step=step):
             state_up(step).wait_send()
 
-        @pl.when((core == 1) & (y >= step))
+        @pl.when((core == 0) & (y >= step))
         def _(step=step):
             state_over(step).wait_send()
 
@@ -852,9 +901,14 @@
     return pl.pallas_call(
         layer_kernel,
         out_shape=jax.ShapeDtypeStruct((32, 6144), BF16),
-        in_specs=[vmem] * 5 + [hbm, vmem, vmem, vmem, vmem, hbm, hbm, hbm],
+        in_specs=[hbm] * 3 + [vmem] * 2 + [hbm] * 2 + [vmem] * 2 + [hbm] * 4,
         out_specs=vmem,
         scratch_shapes=[
+            rows(512, 512),
+            rows(512, 512),
+            rows(512, 512),
+            rows(32, 6144),
+            pltpu.VMEM((EXPERTS, 6144), F32),
             rows(528),
             rows(528),
             pltpu.VMEM((4, 528, 128), BF16),
@@ -866,14 +920,13 @@
             rows(24 * block),
             rows(6 * 2048),
             rows(6 * 1024),
-            rows(6 * 256),
-            rows(6 * 512),
+            rows(6 * 768),
             pltpu.VMEM((EXPERTS, 32, STAGES * UNIT), BF16),
             rows(512, STAGES * UNIT),
-            rows(512, STAGES * UNIT),
+            rows(STAGES * 512),
             rows(block, 512),
             rows(STAGES * block),
-            rows(CAP, 6144),
+            rows(STAGES * block),
             rows(8 * CAP, 6144),
             pltpu.VMEM((8 * CAP, UNIT), F32),
             pltpu.VMEM((8 * CAP, 1152), F32),
@@ -881,9 +934,9 @@
             rows(4 * STAGES * block),
             rows(STAGES * block),
             rows(2 * STAGES * block),
-            rows(block, STAGES * UNIT),
-            pltpu.VMEM((EXPERTS, 32, STAGES * UNIT), BF16),
-            pltpu.SemaphoreType.DMA((7,)),
+            rows(STAGES * block),
+            pltpu.VMEM((STAGES, EXPERTS, 32, UNIT), BF16),
+            pltpu.SemaphoreType.DMA((12,)),
             pltpu.SemaphoreType.DMA((LINKS,)),
             pltpu.SemaphoreType.DMA((LINKS,)),
             pltpu.SemaphoreType.DMA((8,)),

time: 183 us -> 175 us (0.956)
  Pallas kernels: 181 us -> 173 us
    pallas_call x1, Pallas kernels: 181 us -> 173 us  [layer(): pl.pallas_call(layer_kernel, out_shape=jax.ShapeDtypeStruct((32, 6144), B...]
where the time goes in v3:
time: 175 us
  Pallas kernels  173 us (99%)
  local copies, waits for them, and re-layouts  1.77 us (1%)
    pallas_call x1, Pallas kernels, layer(): pl.pallas_call(layer_kernel, out_shape=jax.ShapeDtypeStruct((32, 6144), B...  173 us

profile of v3, /device:TPU:0, one launch (start us, length us, event | category | flops | bytes accessed | tf_op | source)
XLA Modules:
  0.0 174.6 jit_solution(12768003423707033087)
XLA Ops:
  0.0 172.8 %layer.1 = bf16[32,6144]{1,0:T(8,128)(2,1)} custom-call(bf16[512,512]{1,0:T(8,128)(2,1)} %query_ref.1, bf16[512,512]{1,0:T(8,128)(2,1)} %key_ref.1, bf16[512,512]{1,0:T(8,128)(2,1)} %value_ref.1, f32[4,512]{1,0:T(4,128)} %bitcast.17, f32[1,512]{1,0:T(1,128)} %bitcast.19, bf16[512,768]{1,0:T(8,128)(2,1)} %out_w_ref.1, bf16[32,6144]{1,0:T(8,128)(2,1)} %resid_ref.1, ...), custom_call_target="tpu_custom_call" | custom-call | tf_op jit(solution)/shard_map/layer/pallas_call | solution.py:901
  172.8 1.8 %copy.15 = bf16[32,6144]{1,0:T(8,128)(2,1)} copy(bf16[32,6144]{1,0:T(8,128)(2,1)} %layer.1) | data formatting | bytes 786432

commit v4 on v3

--- a/solution.py
+++ b/solution.py
@@ -590,10 +590,13 @@
         gathers[s] = dict(
             up_low=spread(s, ctx, 0, along("y", 1)),
             down_high=spread(s, ctx, 1, along("y", -1)),
-            up_high=spread(s, ctx, 1, along("y", 1)),
-            down_low=spread(s, ctx, 0, along("y", -1)),
             pair=[spread(s, ctx, 2, other_core())],
         )
+
+    def gather_late(s):
+        links.group = "gather"
+        gathers[s]["up_high"] = spread(s, ctx, 1, along("y", 1))
+        gathers[s]["down_low"] = spread(s, ctx, 0, along("y", -1))
 
     from_below, from_above, from_far = below * 2 + core, above * 2 + core, far * 2 + core
 
@@ -674,10 +677,12 @@
     project(2)
     gather(0)
     dispatch(1)
+    gather_late(0)
     relay(2)
     gather_mid(0)
     gather(1)
     turn(2)
+    gather_late(1)
     gather_near(0)
     gather_far(0)
     gather_mid(1)
@@ -756,6 +761,7 @@
     held(2, ("pair",))
     scale_own.wait_recv()
     gate_and_up(2, y)
+    gather_late(2)
     gather_mid(2)
     scale_up.wait_recv()
     scale_on = spread_scale(from_below, along("y", 1))
@@ -779,23 +785,30 @@
     scale_far.wait_recv()
     gate_and_up(2, far)
     sum_far = down(far)
-    for s in range(STAGES):
-        join(far, sum_far, s)
-        rings_y[s].opposite()
+    join(far, sum_far, 0)
+    rings_y[0].opposite()
     held(2, ("near",))
     for made in scale_pair:
         made.wait_recv()
     gate_and_up(2, above)
+    join(far, sum_far, 1)
+    rings_y[1].opposite()
     sum_above = down(above)
+    join(far, sum_far, 2)
+    rings_y[2].opposite()
     gate_and_up(1, below)
     gate_and_up(2, below)
     for s in range(STAGES):
         join(above, sum_above, s)
-        rings_y[s].direct_up()
+        if s < 2:
+            rings_y[s].direct_up()
     sum_below = down(below)
-    for s in range(STAGES):
-        join(below, sum_below, s)
-        rings_y[s].direct_down()
+    join(below, sum_below, 0)
+    rings_y[0].direct_down()
+    rings_y[0].relay()
+    join(below, sum_below, 1)
+    rings_y[1].direct_down()
+    join(below, sum_below, 2)
     for s in range(STAGES):
         join(y, sum_own, s)
 
@@ -829,18 +842,16 @@
     def give_back(s):
         rings_y[s].arrived()
 
-        def one(g, carry):
-            total = rings_y[s].total(g * CAP, CAP).astype(BF16).astype(F32)
-            pieces[rows_at((s * EXPERTS + g) * CAP, CAP), :] = (total * share).astype(BF16)
-            return carry
-
-        lax.fori_loop(0, EXPERTS, one, 0)
         lands = back.at[rows_at((s * EXPERTS + me) * CAP, CAP)]
-        for step in range(1, EXPERTS):
+        for step in list(range(1, EXPERTS)) + [0]:
             to = (me + step) % EXPERTS
+            total = rings_y[s].total(to * CAP, CAP).astype(BF16).astype(F32)
             piece = pieces.at[rows_at((s * EXPERTS + to) * CAP, CAP)]
+            if step == 0:
+                lands[...] = (total * share).astype(BF16)
+                continue
+            piece[...] = (total * share).astype(BF16)
             back_moves[s].append(links.copy(piece, lands, exp_peer(step)))
-        lands[...] = pieces[rows_at((s * EXPERTS + me) * CAP, CAP), :]
 
     def combine(s):
         for made in back_moves[s]:
@@ -856,10 +867,11 @@
             out_moves.append(links.copy(part, rows_out.at[s, me], exp_peer(step)))
         rows_out[s, me] = hidden[rows_at(s * 512 + me * 32, 32), :]
 
-    rings_y[0].relay()
     rings_y[1].relay()
+    rings_y[2].direct_up()
+    rings_y[2].direct_down()
+    give_back(0)
     rings_y[2].relay()
-    give_back(0)
     give_back(1)
     combine(0)
     give_back(2)

time: 175 us -> 171 us (0.977)
  Pallas kernels: 173 us -> 169 us
    pallas_call x1, Pallas kernels: 173 us -> 169 us  [layer(): pl.pallas_call(layer_kernel, out_shape=jax.ShapeDtypeStruct((32, 6144), B...]
where the time goes in v4:
time: 171 us
  Pallas kernels  169 us (99%)
  local copies, waits for them, and re-layouts  1.77 us (1%)
    pallas_call x1, Pallas kernels, layer(): pl.pallas_call(layer_kernel, out_shape=jax.ShapeDtypeStruct((32, 6144), B...  169 us

profile of v4, /device:TPU:0, one launch (start us, length us, event | category | flops | bytes accessed | tf_op | source)
XLA Modules:
  0.0 171.2 jit_solution(15079389751671933056)
XLA Ops:
  0.0 169.4 %layer.1 = bf16[32,6144]{1,0:T(8,128)(2,1)} custom-call(bf16[512,512]{1,0:T(8,128)(2,1)} %query_ref.1, bf16[512,512]{1,0:T(8,128)(2,1)} %key_ref.1, bf16[512,512]{1,0:T(8,128)(2,1)} %value_ref.1, f32[4,512]{1,0:T(4,128)} %bitcast.17, f32[1,512]{1,0:T(1,128)} %bitcast.19, bf16[512,768]{1,0:T(8,128)(2,1)} %out_w_ref.1, bf16[32,6144]{1,0:T(8,128)(2,1)} %resid_ref.1, ...), custom_call_target="tpu_custom_call" | custom-call | tf_op jit(solution)/shard_map/layer/pallas_call | solution.py:913
  169.4 1.8 %copy.15 = bf16[32,6144]{1,0:T(8,128)(2,1)} copy(bf16[32,6144]{1,0:T(8,128)(2,1)} %layer.1) | data formatting | bytes 786432

commit v5 on v4

--- a/solution.py
+++ b/solution.py
@@ -717,7 +717,7 @@
     def owned(owner, chip, s):
         return work.at[rows_at(((owner * 4 + chip) * STAGES + s) * block, block)]
 
-    def down(chip):
+    def down(chip, between=None):
         moves = []
         for s in range(STAGES):
 
@@ -737,6 +737,9 @@
             lax.fori_loop(4 * s, 4 * s + 4, one, 0)
             lands = partner.at[rows_at((chip * STAGES + s) * block, block)]
             moves.append(links.copy(owned(1 - core, chip, s), lands, other_core()))
+            if between is not None and s > 0:
+                join(chip, moves, s - 1)
+                between(s - 1)
         return moves
 
     def join(chip, moves, s):
@@ -784,30 +787,29 @@
     held(2, ("far",))
     scale_far.wait_recv()
     gate_and_up(2, far)
-    sum_far = down(far)
-    join(far, sum_far, 0)
-    rings_y[0].opposite()
+    def far_ready(s):
+        rings_y[s].opposite()
+
+    def above_ready(s):
+        rings_y[s].direct_up()
+
+    def below_ready(s):
+        rings_y[s].direct_down()
+        if s == 0:
+            rings_y[0].relay()
+
+    sum_far = down(far, far_ready)
     held(2, ("near",))
     for made in scale_pair:
         made.wait_recv()
     gate_and_up(2, above)
-    join(far, sum_far, 1)
-    rings_y[1].opposite()
-    sum_above = down(above)
     join(far, sum_far, 2)
     rings_y[2].opposite()
+    sum_above = down(above, above_ready)
     gate_and_up(1, below)
     gate_and_up(2, below)
-    for s in range(STAGES):
-        join(above, sum_above, s)
-        if s < 2:
-            rings_y[s].direct_up()
-    sum_below = down(below)
-    join(below, sum_below, 0)
-    rings_y[0].direct_down()
-    rings_y[0].relay()
-    join(below, sum_below, 1)
-    rings_y[1].direct_down()
+    join(above, sum_above, 2)
+    sum_below = down(below, below_ready)
     join(below, sum_below, 2)
     for s in range(STAGES):
         join(y, sum_own, s)

time: 171 us -> 171 us (level)
  no operation moved by 1% of the time
where the time goes in v5:
time: 171 us
  Pallas kernels  169 us (99%)
  local copies, waits for them, and re-layouts  1.77 us (1%)
    pallas_call x1, Pallas kernels, layer(): pl.pallas_call(layer_kernel, out_shape=jax.ShapeDtypeStruct((32, 6144), B...  169 us

profile of v5, /device:TPU:0, one launch (start us, length us, event | category | flops | bytes accessed | tf_op | source)
XLA Modules:
  0.0 170.7 jit_solution(11151231391462565645)
XLA Ops:
  0.0 168.9 %layer.1 = bf16[32,6144]{1,0:T(8,128)(2,1)} custom-call(bf16[512,512]{1,0:T(8,128)(2,1)} %query_ref.1, bf16[512,512]{1,0:T(8,128)(2,1)} %key_ref.1, bf16[512,512]{1,0:T(8,128)(2,1)} %value_ref.1, f32[4,512]{1,0:T(4,128)} %bitcast.17, f32[1,512]{1,0:T(1,128)} %bitcast.19, bf16[512,768]{1,0:T(8,128)(2,1)} %out_w_ref.1, bf16[32,6144]{1,0:T(8,128)(2,1)} %resid_ref.1, ...), custom_call_target="tpu_custom_call" | custom-call | tf_op jit(solution)/shard_map/layer/pallas_call | solution.py:915
  168.9 1.8 %copy.15 = bf16[32,6144]{1,0:T(8,128)(2,1)} copy(bf16[32,6144]{1,0:T(8,128)(2,1)} %layer.1) | data formatting | bytes 786432
